TPU v7x, 256 devices: a whole 4x4x8 slice. The times are simulated.
256 devices in a mesh: dp: 8 (over y, core), table: 32 (over z, x).
Axes of the slice: x: 4, y: 4, z: 8, core: 2. Of those that a mesh axis runs over, the one named last changes fastest.
Arguments:
- queries: bfloat16 [32768, 768], P(('dp', 'table')), may hold values from -10.2 to 10.2
- tile_ids: int32 [32768, 4], P(('dp', 'table')), may hold values from 0 to 255, as said below
- knowledge: bfloat16 [256, 64, 768], P('table'), may hold values from -6 to 6
- out_proj: bfloat16 [768, 768], replicated, may hold values from -0.21875 to 0.21875
- labels: bfloat16 [64, 512, 768], P('table'), may hold values from -0.21875 to 0.21875
- cluster_ids: int32 [32768, 4], P(('dp', 'table')), may hold values from 0 to 63, all different within a row; in each aligned block of 128 rows (0 to 127, 128 to 255, ...) at most 16 rows name the same one
- positive_picks: int32 [32768, 4], P(('dp', 'table')), may hold values from 0 to 2047
Outputs:
- loss: float32 [32768], P(('dp', 'table'))
- query_grad: float32 [32768, 768], P(('dp', 'table'))
- knowledge_grad: float32 [256, 64, 768], P('table', 'dp')
- label_step: float32 [64, 512, 768], P('table', 'dp')
Inputs may be any that keep to these rules, and one draw needn't show every extreme that they name: `tile_ids`: the queries of one device name at most one distinct tile of each table shard of 8 consecutive tiles; a query may name a tile more than once. `cluster_ids`: each row names 4 different clusters; within the rows of one device no cluster is named by more than 16 rows. `positive_picks`: entry j names label j % 512 of the cluster in column j // 512 of the same row of cluster_ids.
All inputs are finite; a program needn't handle non-finite values.
Results may differ from a plain program's by a relative error of at most 0.015.
Values may be sent and summed in bfloat16 or wider, within the bound.
A program may use at most 128 MiB of HBM per device.

v0:
```python
import math

import jax
import jax.numpy as jnp
from jax import lax
from jax.sharding import PartitionSpec as P

HEADS = 12


logit_ceiling = 10.0
epsilon = 1e-06


def attend(query_rows, key_rows, key_weight):
    row_count, width = query_rows.shape
    head_size = width // HEADS
    query_head_rows = query_rows.reshape(row_count, HEADS, head_size)
    lookup_facet_vectors = key_rows.reshape(key_rows.shape[0], HEADS, head_size)
    scores = jnp.einsum(
        "qrp,zrp->qrz", query_head_rows, lookup_facet_vectors, preferred_element_type=jnp.float32
    ) / math.sqrt(head_size)
    capped = jnp.tanh(scores / logit_ceiling)
    raw_weight = key_weight[:, None, :] * jnp.exp(logit_ceiling * capped)
    soft_weight = raw_weight / jnp.sum(raw_weight, axis=2, keepdims=True)
    smoothed_lower_limit = soft_weight.astype(jnp.bfloat16)
    mixed_heads = jnp.einsum(
        "wvc,cve->wve",
        smoothed_lower_limit,
        lookup_facet_vectors,
        preferred_element_type=jnp.float32,
    )
    return (
        mixed_heads.reshape(row_count, width).astype(jnp.bfloat16),
        soft_weight,
        smoothed_lower_limit,
        capped,
    )


def attend_back(query_rows, key_rows, soft_weight, smoothed_lower_limit, capped, back_proj):
    row_count, width = query_rows.shape
    head_size = width // HEADS
    query_head_rows = query_rows.reshape(row_count, HEADS, head_size)
    lookup_facet_vectors = key_rows.reshape(key_rows.shape[0], HEADS, head_size)
    returned_heads = back_proj.reshape(row_count, HEADS, head_size)
    weight_gradient = jnp.einsum(
        "qrp,zrp->qrz", returned_heads, lookup_facet_vectors, preferred_element_type=jnp.float32
    )
    d_capped = soft_weight * (
        weight_gradient - jnp.sum(soft_weight * weight_gradient, axis=2, keepdims=True)
    )
    logit_derivative = (d_capped * (1.0 - capped * capped) / math.sqrt(head_size)).astype(
        jnp.bfloat16
    )
    d_query = jnp.einsum(
        "wvc,cve->wve", logit_derivative, lookup_facet_vectors, preferred_element_type=jnp.float32
    ).reshape(row_count, width)
    key_gradient = jnp.einsum(
        "qef,qex->fex", logit_derivative, query_head_rows, preferred_element_type=jnp.float32
    )
    key_gradient = key_gradient + jnp.einsum(
        "qef,qex->fex", smoothed_lower_limit, returned_heads, preferred_element_type=jnp.float32
    )
    return (d_query, key_gradient.reshape(key_rows.shape[0], width))


def on_device(queries, tile_ids, knowledge, out_proj, labels, cluster_ids, positive_picks):
    owners = lax.axis_size("table")
    row_count, width = queries.shape
    tiles_here, tile_rows = (knowledge.shape[0], knowledge.shape[1])
    clusters_here, label_count = (labels.shape[0], labels.shape[1])
    shortlist = cluster_ids.shape[1]
    pick_count = positive_picks.shape[1]
    owner_grid = jnp.arange(owners, dtype=jnp.int32)
    owner_hits = (tile_ids // tiles_here)[:, :, None] == owner_grid[None, None, :]
    tile_weight = jnp.sum(owner_hits.astype(jnp.float32), axis=1)
    wanted_tile = (
        jnp.max(jnp.where(owner_hits, (tile_ids % tiles_here)[:, :, None] + 1, 0), axis=(0, 1)) - 1
    )
    asked_tile = lax.all_to_all(
        wanted_tile.reshape(owners, 1), "table", split_axis=0, concat_axis=0, tiled=True
    )[:, 0]
    served = jnp.where(
        (asked_tile >= 0)[:, None, None],
        knowledge[jnp.maximum(asked_tile, 0)],
        jnp.zeros((), jnp.bfloat16),
    )
    key_pool = lax.all_to_all(served, "table", split_axis=0, concat_axis=0, tiled=True)
    key_rows = key_pool.reshape(owners * tile_rows, width)
    key_weight = jnp.broadcast_to(tile_weight[:, :, None], (row_count, owners, tile_rows)).reshape(
        row_count, owners * tile_rows
    )
    mixed_rows, soft_weight, smoothed_lower_limit, capped = attend(queries, key_rows, key_weight)
    augmented = (
        queries.astype(jnp.float32)
        + jnp.dot(mixed_rows, out_proj, preferred_element_type=jnp.float32)
    ).astype(jnp.bfloat16)
    total_clusters = clusters_here * owners
    most_rows = 2 * row_count * shortlist // total_clusters
    slot_total = total_clusters * most_rows
    flat_cluster = cluster_ids.reshape(row_count * shortlist)
    member = (flat_cluster[:, None] == jnp.arange(total_clusters, dtype=jnp.int32)[None, :]).astype(
        jnp.int32
    )
    ordinal_entering = jnp.sum(jnp.cumsum(member, axis=0) * member, axis=1) - 1
    slot_of = flat_cluster * most_rows + ordinal_entering
    source = (
        jnp.zeros((slot_total,), jnp.int32)
        .at[slot_of]
        .set(jnp.arange(row_count * shortlist, dtype=jnp.int32))
    )
    filled = jnp.zeros((slot_total,), jnp.int32).at[slot_of].set(1)
    source_query = source // shortlist
    sent_rows = jnp.where(
        (filled > 0)[:, None], augmented[source_query], jnp.zeros((), jnp.bfloat16)
    )
    pick_ids = positive_picks[source_query]
    wanted_label = jnp.where(
        pick_ids // label_count == (source % shortlist)[:, None], pick_ids % label_count, -1
    )
    sent_ints = jnp.concatenate([wanted_label, filled[:, None]], axis=1)
    got_rows, got_ints = (
        lax.all_to_all(
            sent_rows.reshape(owners, clusters_here, most_rows, width),
            "table",
            split_axis=0,
            concat_axis=0,
            tiled=True,
        ),
        lax.all_to_all(
            sent_ints.reshape(owners, clusters_here, most_rows, pick_count + 1),
            "table",
            split_axis=0,
            concat_axis=0,
            tiled=True,
        ),
    )
    live_mask = got_ints[..., pick_count].astype(jnp.float32)
    label_grid = jnp.arange(label_count, dtype=jnp.int32)
    target = jnp.any(got_ints[..., :pick_count, None] == label_grid, axis=3).astype(jnp.float32)
    logits = jnp.einsum("scmd,cld->scml", got_rows, labels, preferred_element_type=jnp.float32)
    pair_loss = (jnp.sum(jnp.log1p(jnp.exp(logits)) - target * logits, axis=3) * live_mask).astype(
        jnp.bfloat16
    )
    d_logit = ((jax.nn.sigmoid(logits) - target) * live_mask[..., None]).astype(jnp.bfloat16)
    d_pair = jnp.einsum(
        "scml,cld->scmd", d_logit, labels, preferred_element_type=jnp.float32
    ).astype(jnp.bfloat16)
    back_rows, back_loss = (
        lax.all_to_all(d_pair, "table", split_axis=0, concat_axis=0, tiled=True),
        lax.all_to_all(pair_loss, "table", split_axis=0, concat_axis=0, tiled=True),
    )
    pair_rows = back_rows.reshape(slot_total, width)[slot_of].reshape(row_count, shortlist, width)
    d_augment = jnp.sum(pair_rows.astype(jnp.float32), axis=1)
    pair_losses = (
        back_loss.reshape(slot_total)[slot_of].reshape(row_count, shortlist).astype(jnp.float32)
    )
    loss = jnp.sum(pair_losses, axis=1) / (shortlist * label_count)
    back_proj = jnp.einsum(
        "bk,dk->bd", d_augment.astype(jnp.bfloat16), out_proj, preferred_element_type=jnp.float32
    ).astype(jnp.bfloat16)
    d_query, key_gradient = attend_back(
        queries, key_rows, soft_weight, smoothed_lower_limit, capped, back_proj
    )
    query_grad = d_augment + d_query
    returned = lax.all_to_all(
        key_gradient.astype(jnp.bfloat16).reshape(owners, tile_rows, width),
        "table",
        split_axis=0,
        concat_axis=0,
        tiled=True,
    )
    chooser = (asked_tile[None, :] == jnp.arange(tiles_here, dtype=jnp.int32)[:, None]).astype(
        jnp.bfloat16
    )
    tile_total = jnp.einsum("ks,srd->krd", chooser, returned, preferred_element_type=jnp.float32)
    knowledge_grad = lax.psum_scatter(
        tile_total.astype(jnp.bfloat16), "dp", scatter_dimension=1, tiled=True
    ).astype(jnp.float32)
    label_grad = jnp.einsum("scml,scmd->cld", d_logit, got_rows, preferred_element_type=jnp.float32)
    grad_share = lax.psum_scatter(
        label_grad.astype(jnp.bfloat16), "dp", scatter_dimension=1, tiled=True
    ).astype(jnp.float32)
    label_step = grad_share * lax.rsqrt(
        jnp.mean(grad_share * grad_share, axis=2, keepdims=True) + epsilon
    )
    return (loss, query_grad, knowledge_grad, label_step)


def solution(mesh):
    placed = (
        P(("dp", "table"), None),
        P(("dp", "table"), None),
        P("table", None, None),
        P(),
        P("table", None, None),
        P(("dp", "table"), None),
        P(("dp", "table"), None),
    )
    return jax.shard_map(
        on_device,
        mesh=mesh,
        in_specs=placed,
        out_specs=(
            P(("dp", "table")),
            P(("dp", "table"), None),
            P("table", "dp", None),
            P("table", "dp", None),
        ),
        check_vma=False,
    )
```

profile of v0, /device:TPU:16, one launch (start us, length us, event | category | flops | bytes accessed | tf_op | source)
XLA Modules:
  0.0 458.3 jit_solution(10865787624995880012)
XLA Ops:
  8.2 20.8 %all_to_all.36 = s32[32,1,1]{2,1,0:T(1,128)S(1)} all-to-all(s32[32,1,1]{2,1,0:T(1,128)S(1)} %copy.155), channel_id=1, replica_groups=mesh['dp'=8,'table'=32] {'table'}, dimensions={0} | all-to-all | bytes 256 | tf_op jit(solution)/shard_map/all_to_all | solution.py:81
  38.4 4.8 %all-to-all-start.1 = ((bf16[32,64,768]{2,1,0:T(8,128)(2,1)}), bf16[32,64,768]{2,1,0:T(8,128)(2,1)}, u32[]{:S(2)}, u32[]{:S(2)}) async-start(bf16[32,64,768]{2,1,0:T(8,128)(2,1)} %broadcast_select_fusion), calls=%async_computation.1 | async-start | bytes 6291456 | tf_op jit(solution)/shard_map/all_to_all | solution.py:89
  55.7 58.7 %all-to-all-done.1 = bf16[32,64,768]{2,1,0:T(8,128)(2,1)} async-done(((bf16[32,64,768]{2,1,0:T(8,128)(2,1)}), bf16[32,64,768]{2,1,0:T(8,128)(2,1)}, u32[]{:S(2)}, u32[]{:S(2)}) %all-to-all-start.1) | async-done | bytes 3145760 | tf_op jit(solution)/shard_map/all_to_all | solution.py:89
  114.3 6.5 %all-to-all-start.3 = ((s32[32,1,160]{2,1,0:T(1,128)}), s32[32,1,160]{2,1,0:T(1,128)S(1)}, u32[]{:S(2)}, u32[]{:S(2)}) async-start(s32[32,1,160]{2,1,0:T(1,128)} %reshape.229), calls=%async_computation.3 | async-start | bytes 65536 | tf_op jit(solution)/shard_map/all_to_all | solution.py:131
  120.8 10.2 %copy.156 = bf16[32,64,768]{1,0,2:T(8,128)(2,1)} copy(bf16[32,64,768]{2,1,0:T(8,128)(2,1)} %all-to-all-done.1) | data formatting | bytes 6291456 | tf_op jit(solution)/shard_map/all_to_all | solution.py:89
  131.0 9.7 %reshape_reshape.4 = bf16[2048,12,64]{0,2,1:T(8,128)(2,1)} reshape(bf16[32,64,768]{1,0,2:T(8,128)(2,1)} %copy.156) | data formatting | bytes 6291456 | tf_op jit(solution)/shard_map/reshape;reshape | solution.py:19
  140.8 6.1 %fusion.5 = (f32[128,12]{0,1:T(8,128)S(1)}, f32[12,2048,128]{2,1,0:T(8,128)S(1)}) fusion(f32[128,2048]{0,1:T(8,128)S(1)} %bitcast.168, bf16[2048,12,64]{0,2,1:T(8,128)(2,1)} %reshape_reshape.4, bf16[128,12,64]{0,2,1:T(8,128)(2,1)S(1)} %bitcast.179), kind=kOutput, calls=%fused_computation.17 | convolution fusion | flops 415234560 | bytes 16979968 | tf_op jit(solution)/shard_map/qrp,zrp->qrz/dot_general | solution.py:20
  146.9 4.1 fusion.37
  157.3 9.9 %all-to-all-start.2 = ((bf16[32,2,16,768]{3,2,1,0:T(8,128)(2,1)}), bf16[32,2,16,768]{3,2,1,0:T(8,128)(2,1)S(1)}, u32[]{:S(2)}, u32[]{:S(2)}) async-start(bf16[32,2,16,768]{3,2,1,0:T(8,128)(2,1)} %broadcast_select_fusion.1), calls=%async_computation.2 | async-start | bytes 3145728 | tf_op jit(solution)/shard_map/all_to_all | solution.py:124
  172.6 31.2 %all-to-all-done.2 = bf16[32,2,16,768]{3,2,1,0:T(8,128)(2,1)S(1)} async-done(((bf16[32,2,16,768]{3,2,1,0:T(8,128)(2,1)}), bf16[32,2,16,768]{3,2,1,0:T(8,128)(2,1)S(1)}, u32[]{:S(2)}, u32[]{:S(2)}) %all-to-all-start.2) | async-done | bytes 1572896 | tf_op jit(solution)/shard_map/all_to_all | solution.py:124
  203.8 4.0 fusion.18
  210.4 6.2 %all-to-all-start.5 = ((bf16[32,2,16,768]{3,2,1,0:T(8,128)(2,1)}), bf16[32,2,16,768]{3,2,1,0:T(8,128)(2,1)S(1)}, u32[]{:S(2)}, u32[]{:S(2)}) async-start(bf16[32,2,16,768]{3,2,1,0:T(8,128)(2,1)} %copy.171), calls=%async_computation.5 | async-start | bytes 3145728 | tf_op jit(solution)/shard_map/all_to_all | solution.py:151
  216.6 36.3 %all-to-all-done.5 = bf16[32,2,16,768]{3,2,1,0:T(8,128)(2,1)S(1)} async-done(((bf16[32,2,16,768]{3,2,1,0:T(8,128)(2,1)}), bf16[32,2,16,768]{3,2,1,0:T(8,128)(2,1)S(1)}, u32[]{:S(2)}, u32[]{:S(2)}) %all-to-all-start.5) | async-done | bytes 1572896 | tf_op jit(solution)/shard_map/all_to_all | solution.py:151
  257.0 8.4 %fusion.76 = f32[12,2048,128]{2,1,0:T(8,128)} fusion(bf16[2048,12,64]{0,2,1:T(8,128)(2,1)} %reshape_reshape.4, bf16[128,12,64]{0,2,1:T(8,128)(2,1)S(1)} %bitcast.173), kind=kOutput, calls=%fused_computation.129 | convolution fusion | flops 402653184 | bytes 15925248 | tf_op jit(solution)/shard_map/qrp,zrp->qrz/dot_general | solution.py:47
  265.4 26.8 %fusion.14 = f32[12,2048,64]{1,2,0:T(8,128)} fusion(bf16[128,12,64]{0,2,1:T(8,128)(2,1)S(1)} %bitcast.180, f32[12,2048,128]{2,1,0:T(8,128)} %fusion.76, f32[12,2048,128]{2,1,0:T(8,128)} %copy-done.20, f32[128,12]{0,1:T(8,128)S(1)} %get-tuple-element.34, f32[128,2048]{0,1:T(8,128)S(1)} %bitcast.170), kind=kOutput, calls=%fused_computation.30 | convolution fusion | flops 452988416 | bytes 32708608 | tf_op jit(solution)/shard_map/qef,qex->fex/dot_general | solution.py:59
  292.2 9.8 %fusion.7 = bf16[2048,12,64]{0,2,1:T(8,128)(2,1)} fusion(f32[12,2048,64]{1,2,0:T(8,128)} %fusion.14, bf16[128,12,64]{0,2,1:T(8,128)(2,1)S(1)} %bitcast.174, f32[12,2048,128]{2,1,0:T(8,128)} %copy-done.20, f32[128,12]{0,1:T(8,128)S(1)} %get-tuple-element.34, f32[128,2048]{0,1:T(8,128)S(1)} %bitcast.171), kind=kOutput, calls=%fused_computation.21 | convolution fusion | flops 421527552 | bytes 23271424 | tf_op jit(solution)/shard_map/qef,qex->fex/dot_general | solution.py:62
  302.0 10.1 %convert_element_type.112 = bf16[32,64,768]{1,0,2:T(8,128)(2,1)} reshape(bf16[2048,12,64]{0,2,1:T(8,128)(2,1)} %fusion.7) | data formatting | bytes 6291456 | tf_op jit(solution)/shard_map/convert_element_type | solution.py:168
  312.1 8.4 %copy.177 = bf16[32,64,768]{2,1,0:T(8,128)(2,1)} copy(bf16[32,64,768]{1,0,2:T(8,128)(2,1)} %convert_element_type.112) | data formatting | bytes 6291456 | tf_op jit(solution)/shard_map/convert_element_type | solution.py:168
  320.5 5.9 %all-to-all-start.6 = ((bf16[32,64,768]{2,1,0:T(8,128)(2,1)}), bf16[32,64,768]{2,1,0:T(8,128)(2,1)}, u32[]{:S(2)}, u32[]{:S(2)}) async-start(bf16[32,64,768]{2,1,0:T(8,128)(2,1)} %copy.177), calls=%async_computation.6 | async-start | bytes 6291456 | tf_op jit(solution)/shard_map/all_to_all | solution.py:167
  326.5 4.1 bitcast_convert_fusion
  330.7 66.4 %all-to-all-done.6 = bf16[32,64,768]{2,1,0:T(8,128)(2,1)} async-done(((bf16[32,64,768]{2,1,0:T(8,128)(2,1)}), bf16[32,64,768]{2,1,0:T(8,128)(2,1)}, u32[]{:S(2)}, u32[]{:S(2)}) %all-to-all-start.6) | async-done | bytes 3145760 | tf_op jit(solution)/shard_map/all_to_all | solution.py:167
  397.1 5.2 %fusion.31 = bf16[8,64,768]{2,0,1:T(8,128)(2,1)} fusion(bf16[32,64,768]{2,1,0:T(8,128)(2,1)} %all-to-all-done.6, s32[32]{0:T(128)S(1)} %get-tuple-element.28), kind=kOutput, calls=%fused_computation.50 | convolution fusion | flops 25559296 | bytes 3932288 | tf_op jit(solution)/shard_map/ks,srd->krd/dot_general | solution.py:177
  402.4 14.6 %all_to_all.37 = bf16[32,2,16]{2,1,0:T(2,128)(2,1)S(1)} all-to-all(bf16[32,2,16]{2,1,0:T(2,128)(2,1)S(1)} %copy.169), channel_id=1, replica_groups=mesh['dp'=8,'table'=32] {'table'}, dimensions={0} | all-to-all | bytes 4096 | tf_op jit(solution)/shard_map/all_to_all | solution.py:152
  421.3 24.6 %fusion.15 = f32[12,64,128]{2,1,0:T(8,128)S(1)} fusion(bf16[2048,12,64]{0,2,1:T(8,128)(2,1)} %reshape_reshape.4, f32[12,2048,128]{2,1,0:T(8,128)} %fusion.76, f32[12,2048,128]{2,1,0:T(8,128)} %copy-done.20, f32[128,12]{0,1:T(8,128)S(1)} %get-tuple-element.34, f32[128,2048]{0,1:T(8,128)S(1)} %bitcast.172), kind=kOutput, calls=%fused_computation.31 | convolution fusion | flops 452988416 | bytes 29759488 | tf_op jit(solution)/shard_map/wvc,cve->wve/dot_general | solution.py:56
  (124 shorter events, 50.9 us)
Async XLA Ops:
  7.2 196.6 %copy-start = (bf16[2,512,768]{2,1,0:T(8,128)(2,1)S(1)}, bf16[2,512,768]{2,1,0:T(8,128)(2,1)}, u32[]{:S(2)}) copy-start(bf16[2,512,768]{2,1,0:T(8,128)(2,1)} %param.11) | copy-start | bytes 4718596
  34.5 8.7 %copy-start.18 = (s32[128,4]{0,1:T(4,128)S(1)}, s32[128,4]{0,1:T(4,128)}, u32[]{:S(2)}) copy-start(s32[128,4]{0,1:T(4,128)} %param.12) | copy-start | bytes 6148
  34.5 9.3 %copy-start.19 = (s32[128,4]{0,1:T(4,128)S(1)}, s32[128,4]{0,1:T(4,128)}, u32[]{:S(2)}) copy-start(s32[128,4]{0,1:T(4,128)} %param.13) | copy-start | bytes 6148
  34.5 16.3 %copy-start.9 = (bf16[128,768]{1,0:T(8,128)(2,1)S(1)}, bf16[128,768]{1,0:T(8,128)(2,1)}, u32[]{:S(2)}) copy-start(bf16[128,768]{1,0:T(8,128)(2,1)} %param.7) | copy-start | bytes 589828
  38.4 75.9 %all-to-all-start.1 = ((bf16[32,64,768]{2,1,0:T(8,128)(2,1)}), bf16[32,64,768]{2,1,0:T(8,128)(2,1)}, u32[]{:S(2)}, u32[]{:S(2)}) async-start(bf16[32,64,768]{2,1,0:T(8,128)(2,1)} %broadcast_select_fusion), calls=%async_computation.1 | async-start | bytes 6291456 | tf_op jit(solution)/shard_map/all_to_all | solution.py:89
  51.0 89.8 %copy-start.13 = (bf16[128,768]{0,1:T(8,128)(2,1)}, bf16[128,768]{0,1:T(8,128)(2,1)S(1)}, u32[]{:S(2)}) copy-start(bf16[128,768]{0,1:T(8,128)(2,1)S(1)} %copy.157) | copy-start | bytes 589828
  114.3 42.9 %all-to-all-start.3 = ((s32[32,1,160]{2,1,0:T(1,128)}), s32[32,1,160]{2,1,0:T(1,128)S(1)}, u32[]{:S(2)}, u32[]{:S(2)}) async-start(s32[32,1,160]{2,1,0:T(1,128)} %reshape.229), calls=%async_computation.3 | async-start | bytes 65536 | tf_op jit(solution)/shard_map/all_to_all | solution.py:131
  140.8 6.1 %copy-start.7 = (f32[128,32,64]{0,2,1:T(8,128)}, f32[128,32,64]{0,2,1:T(8,128)S(1)}, u32[]{:S(2)}) copy-start(f32[128,32,64]{0,2,1:T(8,128)S(1)} %broadcast_in_dim.79) | copy-start | bytes 3145732
  140.8 6.1 %copy-start.2 = (bf16[2048,12,64]{0,2,1:T(8,128)(2,1)S(1)}, bf16[2048,12,64]{0,2,1:T(8,128)(2,1)}, u32[]{:S(2)}) copy-start(bf16[2048,12,64]{0,2,1:T(8,128)(2,1)} %reshape_reshape.4) | copy-start | bytes 9437188
  157.3 46.5 %all-to-all-start.2 = ((bf16[32,2,16,768]{3,2,1,0:T(8,128)(2,1)}), bf16[32,2,16,768]{3,2,1,0:T(8,128)(2,1)S(1)}, u32[]{:S(2)}, u32[]{:S(2)}) async-start(bf16[32,2,16,768]{3,2,1,0:T(8,128)(2,1)} %broadcast_select_fusion.1), calls=%async_computation.2 | async-start | bytes 3145728 | tf_op jit(solution)/shard_map/all_to_all | solution.py:124
  169.2 39.8 %copy-start.16 = (f32[32,2,16]{2,0,1:T(8,128)}, f32[32,2,16]{2,0,1:T(8,128)S(1)}, u32[]{:S(2)}) copy-start(f32[32,2,16]{2,0,1:T(8,128)S(1)} %fusion.45) | copy-start | bytes 12292
  203.8 5.3 %copy-start.5 = (bf16[32,2,16,768]{3,2,1,0:T(8,128)(2,1)}, bf16[32,2,16,768]{3,2,1,0:T(8,128)(2,1)S(1)}, u32[]{:S(2)}) copy-start(bf16[32,2,16,768]{3,2,1,0:T(8,128)(2,1)S(1)} %all-to-all-done.2) | copy-start | bytes 4718596
  210.4 42.5 %all-to-all-start.5 = ((bf16[32,2,16,768]{3,2,1,0:T(8,128)(2,1)}), bf16[32,2,16,768]{3,2,1,0:T(8,128)(2,1)S(1)}, u32[]{:S(2)}, u32[]{:S(2)}) async-start(bf16[32,2,16,768]{3,2,1,0:T(8,128)(2,1)} %copy.171), calls=%async_computation.5 | async-start | bytes 3145728 | tf_op jit(solution)/shard_map/all_to_all | solution.py:151
  216.6 39.6 %copy-start.4 = (bf16[768,768]{1,0:T(8,128)(2,1)S(1)}, bf16[768,768]{1,0:T(8,128)(2,1)}, u32[]{:S(2)}) copy-start(bf16[768,768]{1,0:T(8,128)(2,1)} %param.10) | copy-start | bytes 3538948
  256.9 8.5 %copy-start.8 = (f32[128,32,64]{0,2,1:T(8,128)S(1)}, f32[128,32,64]{0,2,1:T(8,128)}, u32[]{:S(2)}) copy-start(f32[128,32,64]{0,2,1:T(8,128)} %copy-done.7) | copy-start | bytes 3145732
  257.0 8.4 %copy-start.14 = (bf16[128,768]{0,1:T(8,128)(2,1)S(1)}, bf16[128,768]{0,1:T(8,128)(2,1)}, u32[]{:S(2)}) copy-start(bf16[128,768]{0,1:T(8,128)(2,1)} %copy-done.13) | copy-start | bytes 589828
  312.1 14.4 %copy-start.6 = (bf16[32,2,16,768]{3,2,1,0:T(8,128)(2,1)S(1)}, bf16[32,2,16,768]{3,2,1,0:T(8,128)(2,1)}, u32[]{:S(2)}) copy-start(bf16[32,2,16,768]{3,2,1,0:T(8,128)(2,1)} %copy-done.5) | copy-start | bytes 4718596
  312.1 14.4 %copy-start.17 = (f32[32,2,16]{2,0,1:T(8,128)S(1)}, f32[32,2,16]{2,0,1:T(8,128)}, u32[]{:S(2)}) copy-start(f32[32,2,16]{2,0,1:T(8,128)} %copy-done.16) | copy-start | bytes 12292
  320.5 76.6 %all-to-all-start.6 = ((bf16[32,64,768]{2,1,0:T(8,128)(2,1)}), bf16[32,64,768]{2,1,0:T(8,128)(2,1)}, u32[]{:S(2)}, u32[]{:S(2)}) async-start(bf16[32,64,768]{2,1,0:T(8,128)(2,1)} %copy.177), calls=%async_computation.6 | async-start | bytes 6291456 | tf_op jit(solution)/shard_map/all_to_all | solution.py:167
  326.4 120.5 %reduce-scatter.5.cloned.1.call-start = ((), (), s32[]{:S(2)}) async-start(), calls=%async_computation.10 | async-start | bytes 1769472 | tf_op jit(solution)/shard_map/reduce_scatter | solution.py:182
  330.6 71.7 %copy-start.12 = (s32[32,2,16,1]{2,1,3,0:T(2,128)S(1)}, s32[32,2,16,1]{2,1,3,0:T(2,128)}, u32[]{:S(2)}) copy-start(s32[32,2,16,1]{2,1,3,0:T(2,128)} %copy-done.11) | copy-start | bytes 12292
  330.6 71.7 %copy-start.15 = (f32[32,2,16]{2,0,1:T(8,128)S(1)}, f32[32,2,16]{2,0,1:T(8,128)}, u32[]{:S(2)}) copy-start(f32[32,2,16]{2,0,1:T(8,128)} %get-tuple-element.36) | copy-start | bytes 12292
  330.6 119.1 %reduce-scatter.3.cloned.1.call-start = ((), (), s32[]{:S(2)}) async-start(), calls=%async_computation.9 | async-start | bytes 884736 | tf_op jit(solution)/shard_map/reduce_scatter | solution.py:178
  421.3 30.0 %copy-start.1 = (bf16[2,512,768]{2,1,0:T(8,128)(2,1)S(1)}, bf16[2,512,768]{2,1,0:T(8,128)(2,1)}, u32[]{:S(2)}) copy-start(bf16[2,512,768]{2,1,0:T(8,128)(2,1)} %param.11) | copy-start | bytes 4718596
  (5 other events, 15.1 us)
Sparse Core Ops, SparseCore 0:
  330.7 31.5 reduce-scatter.4
  402.4 25.4 reduce-scatter.2
where the time goes:
time: 465 us; the launch traced here: 458 us
  waiting for transfers between devices  193 us (42%)
  matrix products  95.2 us (20%)
  local copies, waits for them, and re-layouts  67.7 us (15%)
  blocking collectives  35.4 us (8%)
  starting transfers between devices  33.3 us (7%)
  other arithmetic  19.4 us (4%)
  between operations  14.8 us (3%)
    all_to_all x1, waiting for transfers between devices, on_device(): lax.all_to_all(key_gradient.astype(jnp.bfloat16).reshape(owners, tile_row...  66.4 us
    all_to_all x1, waiting for transfers between devices, on_device(): lax.all_to_all(served, 'table', split_axis=0, concat_axis=0, tiled=True)  58.7 us
    all_to_all x1, waiting for transfers between devices, on_device(): lax.all_to_all(d_pair, 'table', split_axis=0, concat_axis=0, tiled=True)  36.3 us
    all_to_all x1, waiting for transfers between devices, on_device(): lax.all_to_all(sent_rows.reshape(owners, clusters_here, most_rows, width)...  31.2 us
    dot_general x1, matrix products, attend_back(): jnp.einsum('qef,qex->fex', logit_derivative, query_head_rows, preferred_e...  26.8 us
    dot_general x1, matrix products, attend_back(): jnp.einsum('wvc,cve->wve', logit_derivative, lookup_facet_vectors, prefer...  24.6 us
    all_to_all x1, blocking collectives, on_device(): lax.all_to_all(wanted_tile.reshape(owners, 1), 'table', split_axis=0, con...  20.8 us
    convert_element_type x2, local copies, waits for them, and re-layouts, on_device(): key_gradient.astype(jnp.bfloat16).reshape(owners, tile_rows, width)  18.5 us
  transfers between devices with their start and end apart: 7, of which 4 were waited for; matrix products, arithmetic and copies ran while one was open for 21% of the time, Pallas kernels for 0%

commit v1 on v0

v1 whole, which is shorter than its diff:
```python
import functools
import math

import jax
import jax.numpy as jnp
from jax import lax
from jax.experimental import pallas as pl
from jax.experimental.pallas import tpu as pltpu
from jax.sharding import PartitionSpec as P

MESH = pl.DeviceIdType.MESH
DMA = pltpu.SemaphoreType.DMA
F32 = jnp.float32
BF16 = jnp.bfloat16
HEADS = 12
PAIRS = 6
Q = 128
D = 768
NZ = 8
NX = 4
NY = 4
epsilon = 1e-06
LOG2E = 1.4426950408889634
VMEM_LIMIT = 50 << 20


def where_am_i():
    dp, t = lax.axis_index("dp"), lax.axis_index("table")
    return dp // 2, dp % 2, t // NX, t % NX


def dev(y, c, z, x):
    return (y * 2 + c, z * NX + x)


def greet(peers):
    barrier = pltpu.get_barrier_semaphore()
    for peer in peers:
        pl.semaphore_signal(barrier, inc=1, device_id=peer, device_id_type=MESH)
    pl.semaphore_wait(barrier, len(peers))


def remote(src, dst, send, recv, to):
    return pltpu.make_async_remote_copy(
        src_ref=src, dst_ref=dst, send_sem=send, recv_sem=recv, device_id=to, device_id_type=MESH
    )


def nt(a, b):
    return lax.dot_general(a, b, (((1,), (1,)), ((), ())), preferred_element_type=F32)


def tn(a, b):
    return lax.dot_general(a, b, (((0,), (0,)), ((), ())), preferred_element_type=F32)


def nn(a, b):
    return jnp.dot(a, b, preferred_element_type=F32)


def stack_heads(rows, stacked_ref):
    lane = lax.broadcasted_iota(jnp.int32, (Q, 128), 1)
    for p in range(PAIRS):
        part = rows[:, p * 128 : (p + 1) * 128]
        stacked_ref[p, :Q] = jnp.where(lane < 64, part, jnp.zeros_like(part))
        stacked_ref[p, Q:] = jnp.where(lane < 64, jnp.zeros_like(part), part)


def unstack_heads(both):
    return jnp.concatenate([both[0:64, 0:Q], both[64:128, Q : 2 * Q]], axis=0)


def weight_block(tw):
    tw2 = jnp.concatenate([tw, tw], axis=1)
    return jnp.broadcast_to(tw2[:, None, :], (NX, 64, 2 * Q)).reshape(NX * 64, 2 * Q)


XC = [(dx, dc) for dx in range(NX) for dc in range(2)]


def keys_kernel(
    know, wanted, queries, tile_weight, out_proj, msg,
    keys, aug, mixed_t, total, asks, ints,
    half, r0, r1, r2, l0, l1, l2, far, stage, stacked, acc, mid,
    ask_smem, z_send, z_recv, x_send, x_recv, a_send, a_recv, m_send, m_recv, n_send, n_recv, l_sem,
):
    y, c, z, x = where_am_i()
    me = x * 2 + c
    right, left = dev(y, c, (z + 1) % NZ, x), dev(y, c, (z + NZ - 1) % NZ, x)
    group = [((x + dx) % NX, (c + dc) % 2) for dx, dc in XC]
    greet(
        [dev(y, pc, z, px) for px, pc in group[1:]]
        + [dev(y, c, (z + d) % NZ, x) for d in range(1, NZ)]
    )
    half[...] = know[:, pl.ds(pl.multiple_of(c * 32, 32), 32), :]
    ask_copies = []
    for j in range(1, 8):
        px, pc = group[j]
        cp = remote(wanted, asks.at[me], a_send.at[j], a_recv.at[j], dev(y, pc, z, px))
        cp.start()
        ask_copies.append(cp)
    ring = {}
    slots = ((half, r0, r1, r2, far), (half, l0, l1, l2, far))

    def ring_send(way, step, k):
        piece = pl.ds(k * 2, 2)
        cp = remote(
            slots[way][step].at[piece], slots[way][step + 1].at[piece],
            z_send.at[way, step, k], z_recv.at[way, step, k], right if way == 0 else left,
        )
        cp.start()
        ring[way, step, k] = cp

    for k in range(4):
        for way in (0, 1):
            ring_send(way, 0, k)
    m_copies = []
    for dx in range(1, NX):
        px = (x + dx) % NX
        cp = remote(msg.at[px], mid.at[x], m_send.at[dx], m_recv.at[dx], dev(y, c, z, px))
        cp.start()
        m_copies.append(cp)
    asks[me] = wanted[...]
    mid[x] = msg[x]
    stack_heads(queries[...], stacked)
    acc[...] = jnp.zeros_like(acc)
    total[...] = jnp.zeros_like(total)
    for cp in ask_copies:
        cp.wait()
    cp = pltpu.make_async_copy(asks, ask_smem, l_sem)
    cp.start()
    cp.wait()
    sent = []

    def serve(zo, shard):
        row = pl.ds(pl.multiple_of(c * 32, 32), 32)
        for j, (px, pc) in enumerate(group):
            tile = ask_smem[px * 2 + pc, zo, x]
            if j == 0:
                keys[zo * NX + x, row] = shard[tile]
                continue
            stage[j, zo] = shard[tile]
            cp = remote(
                stage.at[j, zo], keys.at[zo * NX + x, row], x_send.at[j, zo], x_recv.at[j, zo],
                dev(y, pc, z, px),
            )
            cp.start()
            sent.append(cp)

    def arrived(zo):
        for j in range(1, 8):
            row = pl.ds(0, 32)
            remote(
                stage.at[j, zo], keys.at[zo * NX, row], x_send.at[j, zo], x_recv.at[j, zo], right
            ).wait_recv()

    def attend(zo):
        w = weight_block(tile_weight[zo])

        def pair(p, carry):
            lanes = pl.ds(pl.multiple_of(p * 128, 128), 128)
            k = keys[pl.ds(zo * NX, NX), :, lanes].reshape(256, 128)
            capped = jnp.tanh(nt(k, stacked[p]) * (1.0 / 80.0))
            raw = w * jnp.exp2(capped * (10.0 * LOG2E))
            total[p] = total[p] + jnp.sum(raw, axis=0, keepdims=True)
            acc[p] = acc[p] + tn(k, raw.astype(BF16))
            return carry

        lax.fori_loop(0, PAIRS, pair, 0)

    def wait_step(way, step, k):
        ring[way, step, k].wait_recv()

    serve(z, half)
    for cp in m_copies:
        cp.wait()
    n_copies = []
    for d in range(1, NZ):
        zp = (z + d) % NZ
        cp = remote(
            mid.at[:, zp], ints.at[z], n_send.at[d], n_recv.at[d], dev(y, c, zp, x)
        )
        cp.start()
        n_copies.append(cp)
    ints[z] = mid[:, z]
    pending = [z]
    for step in range(1, 4):
        for k in range(4):
            for way in (0, 1):
                wait_step(way, step - 1, k)
                if step < 3 or (k < 2) == (way == 0):
                    ring_send(way, step, k)
        serve((z + NZ - step) % NZ, slots[0][step])
        serve((z + step) % NZ, slots[1][step])
        for zo in pending:
            arrived(zo)
            attend(zo)
        pending = [(z + NZ - step) % NZ, (z + step) % NZ]
    for k in range(4):
        wait_step(0 if k < 2 else 1, 3, k)
    serve((z + 4) % NZ, far)
    for zo in pending:
        arrived(zo)
        attend(zo)
    for cp in n_copies:
        cp.wait()
    arrived((z + 4) % NZ)
    attend((z + 4) % NZ)
    for p in range(PAIRS):
        mixed_t[p] = unstack_heads(acc[p] / total[p])
    mixed = jnp.concatenate([mixed_t[p].T for p in range(PAIRS)], axis=1).astype(BF16)
    aug[...] = (queries[...].astype(F32) + nn(mixed, out_proj[...])).astype(BF16)
    for cp in ring.values():
        cp.wait_send()
    for cp in sent:
        cp.wait_send()


def labels_kernel(
    aug, ints, wcol, labels,
    d_aug, loss, label_grad,
    rows, served, got, back, back_got, lstage, lgot, dlogit, onehot, lpart, lsend, lrecv,
    psend, prbuf,
    z_send, z_recv, x_send, x_recv, b_send, b_recv, s_send, s_recv, p_send, p_recv, q_send, q_recv,
):
    y, c, z, x = where_am_i()
    right, left = dev(y, c, (z + 1) % NZ, x), dev(y, c, (z + NZ - 1) % NZ, x)
    greet(
        [dev(y, c, z, (x + dx) % NX) for dx in range(1, NX)]
        + [dev(y, c, (z + d) % NZ, x) for d in range(1, NZ)]
    )
    ring = {}

    def ring_send(way, step, k):
        own = (z + NZ - step) % NZ if way == 0 else (z + step) % NZ
        piece = pl.ds(k * 32, 32)
        src = aug.at[piece] if step == 0 else rows.at[own, piece]
        cp = remote(
            src, rows.at[own, piece], z_send.at[way, step, k], z_recv.at[way, step, k],
            right if way == 0 else left,
        )
        cp.start()
        ring[way, step, k] = cp

    for k in range(4):
        for way in (0, 1):
            ring_send(way, 0, k)
    rows[z] = aug[...]
    query = lax.broadcasted_iota(jnp.int32, (Q, 128), 0)

    def hot(i, carry):
        onehot[i] = jnp.where(query == ints[i, x, 5:6, :], 1.0, 0.0).astype(BF16)
        return carry

    lax.fori_loop(0, NZ, hot, 0)
    sent = []

    def serve(zs):
        picked = tn(onehot[zs], rows[zs]).astype(BF16)
        served[zs] = picked.reshape(NX, 2, 16, D)
        got[x, :, zs] = served[zs, x]
        for dx in range(1, NX):
            px = (x + dx) % NX
            cp = remote(
                served.at[zs, px], got.at[x, :, zs], x_send.at[dx, zs], x_recv.at[dx, zs],
                dev(y, c, z, px),
            )
            cp.start()
            sent.append(cp)

    serve(z)
    for step in range(1, 4):
        for k in range(4):
            for way in (0, 1):
                ring[way, step - 1, k].wait_recv()
                if step < 3 or (k < 2) == (way == 0):
                    ring_send(way, step, k)
        serve((z + NZ - step) % NZ)
        serve((z + step) % NZ)
    for k in range(4):
        ring[0 if k < 2 else 1, 3, k].wait_recv()
    serve((z + 4) % NZ)
    label = lax.broadcasted_iota(jnp.int32, (128, 512), 1)
    lane = lax.broadcasted_iota(jnp.int32, (NZ, 16, 128), 2)
    source = lax.broadcasted_iota(jnp.int32, (NZ, 16, 128), 0)

    def work(xs):
        def cluster(cl, carry):
            entries = got[xs, cl].reshape(128, D)
            logits = nt(entries, labels[cl])
            want = wcol[xs * 2 + cl]
            live = (want[:, 4:5] > 0).astype(F32)
            hit = label == want[:, 0:1]
            for j in range(1, 4):
                hit = hit | (label == want[:, j : j + 1])
            e = jnp.exp(-jnp.abs(logits))
            soft = jnp.maximum(logits, 0.0) + jnp.log1p(e)
            pair_loss = jnp.sum(soft - jnp.where(hit, logits, 0.0), axis=1, keepdims=True) * live
            inv = 1.0 / (1.0 + e)
            sig = jnp.where(logits >= 0, inv, 1.0 - inv)
            dl = ((sig - jnp.where(hit, 1.0, 0.0)) * live).astype(BF16)
            dlogit[cl, xs] = dl
            back[xs, cl] = nn(dl, labels[cl]).astype(BF16).reshape(NZ, 16, D)
            spread = jnp.broadcast_to(pair_loss, (128, 128)).reshape(NZ, 16, 128)
            lstage[xs, cl] = jnp.sum(jnp.where(lane == source, spread, 0.0), axis=0)
            return carry

        lax.fori_loop(0, 2, cluster, 0)

    back_copies = []
    for dx in (0, 1, 3, 2):
        xs = (x + NX - dx) % NX
        if dx:
            for zs in range(NZ):
                remote(
                    served.at[0, 0], got.at[xs, :, 0], x_send.at[dx, zs], x_recv.at[dx, zs], right
                ).wait_recv()
        work(xs)
        if dx == 0:
            back_got[x] = back[x]
            lgot[x] = lstage[x]
        else:
            to = dev(y, c, z, xs)
            for cp in (
                remote(back.at[xs], back_got.at[x], b_send.at[dx], b_recv.at[dx], to),
                remote(lstage.at[xs], lgot.at[x], s_send.at[dx], s_recv.at[dx], to),
            ):
                cp.start()
                back_copies.append(cp)
    for cl in range(2):
        label_grad[cl] = tn(
            dlogit[cl].reshape(512, 512), got[:, cl].reshape(512, D)
        ).astype(BF16)
    for cp in back_copies:
        cp.wait()

    def partial(zs):
        pairs = back_got[:, :, zs].reshape(128, D)
        return nn(onehot[zs], pairs)

    p_copies = []

    def chain_send(way, step, value, dest_rows):
        psend[way, step, dest_rows] = value.astype(BF16)
        cp = remote(
            psend.at[way, step, dest_rows], prbuf.at[way, step, dest_rows],
            p_send.at[way, step], p_recv.at[way, step], right if way == 0 else left,
        )
        cp.start()
        p_copies.append(cp)
        return cp

    low, high, whole = pl.ds(0, 64), pl.ds(64, 64), pl.ds(0, Q)
    far = partial((z + 4) % NZ)
    previous = [chain_send(0, 0, far[:64], low), chain_send(1, 0, far[64:], high)]
    losses = jnp.concatenate([lgot[i].reshape(32, 128) for i in range(NX)], axis=0).astype(BF16)
    out_lane = lax.broadcasted_iota(jnp.int32, (Q, 128), 1)
    lpart[...] = jnp.zeros_like(lpart)

    def loss_of(i, carry):
        lpart[...] = lpart[...] + jnp.where(out_lane == i, nn(onehot[i], losses), 0.0)
        return carry

    lax.fori_loop(0, NZ, loss_of, 0)
    lsend[...] = lpart[...].T[:NZ]
    l_copies = []
    for d in range(1, NZ):
        zp = (z + d) % NZ
        cp = remote(lsend, lrecv.at[z], q_send.at[d], q_recv.at[d], dev(y, c, zp, x))
        cp.start()
        l_copies.append(cp)
    lrecv[z] = lsend[...]
    for step in range(1, 4):
        d = 4 - step
        to_right, to_left = partial((z + d) % NZ), partial((z + NZ - d) % NZ)
        for cp in previous:
            cp.wait_recv()
        if step == 1:
            zeros = jnp.zeros((64, D), F32)
            in_right = jnp.concatenate([prbuf[0, 0, :64].astype(F32), zeros], axis=0)
            in_left = jnp.concatenate([zeros, prbuf[1, 0, 64:].astype(F32)], axis=0)
        else:
            in_right, in_left = prbuf[0, step - 1].astype(F32), prbuf[1, step - 1].astype(F32)
        previous = [
            chain_send(0, step, to_right + in_right, whole),
            chain_send(1, step, to_left + in_left, whole),
        ]
    mine = partial(z)
    for cp in previous:
        cp.wait_recv()
    d_aug[...] = mine + prbuf[0, 3].astype(F32) + prbuf[1, 3].astype(F32)
    for cp in l_copies:
        cp.wait()
    loss[...] = jnp.sum(lrecv[:, pl.ds(z, 1), :], axis=0) * (1.0 / 2048.0)
    for cp in p_copies:
        cp.wait_send()
    for cp in ring.values():
        cp.wait_send()
    for cp in sent:
        cp.wait_send()


def grads_kernel(
    asks, keys, queries, d_aug, out_proj, mixed_t, total, tile_weight,
    query_grad, know_grad,
    stacked, d_acc, delta, gsend, ggot, ysend, ygot, zsend, zgot,
    x_send, x_recv, y_send, y_recv, z_send, z_recv,
):
    y, c, z, x = where_am_i()
    me = x * 2 + c
    group = [((x + dx) % NX, (c + dc) % 2) for dx, dc in XC]
    greet(
        [dev(y, pc, z, px) for px, pc in group[1:]]
        + [dev((y + d) % NY, c, z, x) for d in range(1, NY)]
        + [dev(y, c, (z + d) % NZ, x) for d in range(1, NZ)]
    )
    d_rows = d_aug[...]
    back_proj = nt(d_rows.astype(BF16), out_proj[...]).astype(BF16)
    stack_heads(queries[...], stacked.at[:, 0:256])
    stack_heads(back_proj, stacked.at[:, 256:512])
    for p in range(PAIRS):
        product = mixed_t[p] * back_proj[:, p * 128 : (p + 1) * 128].astype(F32).T
        delta[p] = jnp.concatenate(
            [
                jnp.sum(product[:64], axis=0, keepdims=True),
                jnp.sum(product[64:], axis=0, keepdims=True),
            ],
            axis=1,
        )
    d_acc[...] = jnp.zeros_like(d_acc)

    def compute(zo):
        w = weight_block(tile_weight[zo])

        def pair(p, carry):
            lanes = pl.ds(pl.multiple_of(p * 128, 128), 128)
            k = keys[pl.ds(zo * NX, NX), :, lanes].reshape(256, 128)
            rows = stacked[p]
            products = nt(k, rows)
            capped = jnp.tanh(products[:, :256] * (1.0 / 80.0))
            soft = w * jnp.exp2(capped * (10.0 * LOG2E)) * (1.0 / total[p])
            d_score = soft * (products[:, 256:] - delta[p]) * ((1.0 - capped * capped) * 0.125)
            both = jnp.concatenate([d_score.astype(BF16), soft.astype(BF16)], axis=1)
            d_acc[p] = d_acc[p] + tn(k, both[:, :256])
            grad = nn(both, rows).reshape(NX, NY, 2, 8, 128)
            for side in range(2):
                gsend[zo, :, side, :, lanes] = grad[:, :, side].reshape(NX, 32, 128).astype(BF16)
            return carry

        lax.fori_loop(0, PAIRS, pair, 0)
        ggot[me, zo] = gsend[zo, x, c]
        for j in range(1, 8):
            px, pc = group[j]
            remote(
                gsend.at[zo, px, pc], ggot.at[me, zo], x_send.at[j, zo], x_recv.at[j, zo],
                dev(y, pc, z, px),
            ).start()

    def gather_tiles(zo):
        for j in range(1, 8):
            remote(
                gsend.at[zo, 0, 0], ggot.at[0, zo], x_send.at[j, zo], x_recv.at[j, zo],
                dev(y, c, z, x),
            ).wait_recv()
        tiles = [asks[s, zo, x] for s in range(8)]

        def two_tiles(k2, carry):
            sums = []
            for k in range(2):
                value = jnp.zeros((32, D), F32)
                for s in range(8):
                    value = value + ggot[s, zo].astype(F32) * jnp.where(
                        tiles[s] == k2 * 2 + k, 1.0, 0.0
                    )
                sums.append(value.reshape(NY, 1, 8, D))
            joined = jnp.concatenate(sums, axis=1).reshape(NY, 16, D).astype(BF16)
            ysend[zo, :, k2] = joined
            return carry

        lax.fori_loop(0, 4, two_tiles, 0)
        ygot[y, zo] = ysend[zo, y]
        for d in range(1, NY):
            py = (y + d) % NY
            remote(
                ysend.at[zo, py], ygot.at[y, zo], y_send.at[d, zo], y_recv.at[d, zo],
                dev(py, c, z, x),
            ).start()

    def gather_shards(zo, own):
        for d in range(1, NY):
            remote(
                ysend.at[zo, 0], ygot.at[0, zo], y_send.at[d, zo], y_recv.at[d, zo],
                dev(y, c, z, x),
            ).wait_recv()
        value = ygot[0, zo].astype(F32)
        for i in range(1, NY):
            value = value + ygot[i, zo].astype(F32)
        zsend[zo] = value.astype(BF16)

        @pl.when(own == 0)
        def _():
            zgot[z] = zsend[z]

        @pl.when(own != 0)
        def _():
            remote(
                zsend.at[zo], zgot.at[z], z_send.at[own], z_recv.at[own], dev(y, c, zo, x)
            ).start()

    def offset(i):
        return (3 * (i + 1)) % NZ

    def body(i, carry):
        @pl.when(i < 8)
        def _():
            compute((z + offset(i)) % NZ)

        @pl.when((i >= 1) & (i < 9))
        def _():
            gather_tiles((z + offset(i - 1)) % NZ)

        @pl.when(i >= 2)
        def _():
            gather_shards((z + offset(i - 2)) % NZ, offset(i - 2))

        return carry

    lax.fori_loop(0, 10, body, 0)
    d_query = jnp.concatenate([unstack_heads(d_acc[p]).T for p in range(PAIRS)], axis=1)
    query_grad[...] = d_rows + d_query
    for d in range(1, NZ):
        remote(zsend.at[0], zgot.at[0], z_send.at[d], z_recv.at[d], dev(y, c, z, x)).wait_recv()
    value = zgot[0].astype(F32)
    for i in range(1, NZ):
        value = value + zgot[i].astype(F32)
    know_grad[...] = value.reshape(8, 8, D)

    def drain(zo, carry):
        for j in range(1, 8):
            remote(
                gsend.at[zo, 0, 0], ggot.at[0, zo], x_send.at[j, zo], x_recv.at[j, zo],
                dev(y, c, z, x),
            ).wait_send()
        for d in range(1, NY):
            remote(
                ysend.at[zo, 0], ygot.at[0, zo], y_send.at[d, zo], y_recv.at[d, zo],
                dev(y, c, z, x),
            ).wait_send()
        return carry

    lax.fori_loop(0, NZ, drain, 0)
    for d in range(1, NZ):
        remote(zsend.at[0], zgot.at[0], z_send.at[d], z_recv.at[d], dev(y, c, z, x)).wait_send()


V = pl.BlockSpec(memory_space=pltpu.VMEM)
S = pl.BlockSpec(memory_space=pltpu.SMEM)


def run(kernel, number, outs, scratch, *args, in_specs=None):
    return pl.pallas_call(
        kernel,
        out_shape=[jax.ShapeDtypeStruct(shape, dtype) for shape, dtype in outs],
        in_specs=in_specs or [V] * len(args),
        out_specs=[V] * len(outs),
        scratch_shapes=scratch,
        compiler_params=pltpu.CompilerParams(
            collective_id=number, has_side_effects=True, vmem_limit_bytes=VMEM_LIMIT
        ),
        cost_estimate=pl.CostEstimate(
            flops=4_000_000_000, bytes_accessed=40_000_000, transcendentals=6_000_000
        ),
    )(*args)


def prepare(tile_ids, cluster_ids, positive_picks):
    tiles, ids, picks = tile_ids.T, cluster_ids.T, positive_picks.T
    owner = jnp.arange(32, dtype=jnp.int32)
    hits = (tiles // 8)[:, None, :] == owner[None, :, None]
    tile_weight = jnp.sum(hits.astype(F32), axis=0)
    wanted = jnp.max(jnp.where(hits, (tiles % 8)[:, None, :], 0), axis=(0, 2))
    wanted = jnp.pad(wanted.reshape(NZ, NX), ((0, 0), (0, 128 - NX)))
    cluster = jnp.arange(64, dtype=jnp.int32)
    member = jnp.any(ids[:, None, :] == cluster[None, :, None], axis=0)
    before = (jnp.arange(Q)[:, None] < jnp.arange(Q)[None, :]).astype(BF16)
    rank = jnp.dot(member.astype(BF16), before, preferred_element_type=F32).astype(jnp.int32)
    rank = jnp.where(member, rank, -1)
    slot = jnp.arange(16, dtype=jnp.int32)
    held = rank[:, None, :] == slot[None, :, None]
    query = jnp.arange(Q, dtype=jnp.int32)
    slot_query = Q + jnp.sum(jnp.where(held, query - Q, 0), axis=2)
    live = (slot_query < Q).astype(jnp.int32)
    column = picks // 512
    pick_cluster = jnp.sum(
        jnp.where(column[:, None, :] == jnp.arange(4)[None, :, None], ids[None], 0), axis=1
    )
    pick_label = picks % 512 + 1
    wanted_label = [
        jnp.sum(
            jnp.where(
                held & (pick_cluster[j][None, None, :] == cluster[:, None, None]),
                pick_label[j],
                0,
            ),
            axis=2,
        )
        - 1
        for j in range(4)
    ]
    parts = [a.reshape(NZ, NX, 1, 32) for a in wanted_label + [live]]
    parts = jnp.pad(jnp.concatenate(parts, axis=2), ((0, 0), (0, 0), (0, 0), (0, 96)))
    slots = jnp.broadcast_to(slot_query.reshape(NZ, 1, 1, 128), (NZ, NX, 1, 128))
    msg = jnp.concatenate([parts, slots, jnp.zeros((NZ, NX, 2, 128), jnp.int32)], axis=2)
    return tile_weight.reshape(NZ, NX, Q), wanted, msg.transpose(1, 0, 2, 3)


def on_device(queries, tile_ids, knowledge, out_proj, labels, cluster_ids, positive_picks):
    tile_weight, wanted, msg = prepare(tile_ids, cluster_ids, positive_picks)
    keys, aug, mixed_t, total, asks, ints = run(
        keys_kernel,
        1,
        [
            ((32, 64, D), BF16),
            ((Q, D), BF16),
            ((PAIRS, 128, Q), F32),
            ((PAIRS, 1, 2 * Q), F32),
            ((8, 8, 128), jnp.int32),
            ((NZ, NX, 8, 128), jnp.int32),
        ],
        [
            *[pltpu.VMEM((8, 32, D), BF16) for _ in range(8)],
            pltpu.VMEM((8, NZ, 32, D), BF16),
            pltpu.VMEM((PAIRS, 2 * Q, 128), BF16),
            pltpu.VMEM((PAIRS, 128, 2 * Q), F32),
            pltpu.VMEM((NX, NZ, 8, 128), jnp.int32),
            pltpu.SMEM((8, 8, 128), jnp.int32),
            DMA((2, 4, 4)),
            DMA((2, 4, 4)),
            DMA((8, NZ)),
            DMA((8, NZ)),
            DMA((8,)),
            DMA((8,)),
            DMA((NX,)),
            DMA((NX,)),
            DMA((NZ,)),
            DMA((NZ,)),
            DMA,
        ],
        knowledge, wanted, queries, tile_weight, out_proj, msg,
    )
    wcol = ints[:, :, :5, :32].reshape(NZ, NX, 5, 2, 16).transpose(1, 3, 0, 4, 2)
    wcol = jnp.pad(wcol.reshape(8, 128, 5), ((0, 0), (0, 0), (0, 3)))
    d_aug, loss, label_grad = run(
        labels_kernel,
        2,
        [((Q, D), F32), ((1, Q), F32), ((2, 512, D), BF16)],
        [
            pltpu.VMEM((NZ, Q, D), BF16),
            pltpu.VMEM((NZ, NX, 2, 16, D), BF16),
            pltpu.VMEM((NX, 2, NZ, 16, D), BF16),
            pltpu.VMEM((NX, 2, NZ, 16, D), BF16),
            pltpu.VMEM((NX, 2, NZ, 16, D), BF16),
            pltpu.VMEM((NX, 2, 16, 128), F32),
            pltpu.VMEM((NX, 2, 16, 128), F32),
            pltpu.VMEM((2, NX, 128, 512), BF16),
            pltpu.VMEM((NZ, Q, 128), BF16),
            pltpu.VMEM((Q, 128), F32),
            pltpu.VMEM((NZ, 128), F32),
            pltpu.VMEM((NZ, NZ, 128), F32),
            pltpu.VMEM((2, 4, Q, D), BF16),
            pltpu.VMEM((2, 4, Q, D), BF16),
            DMA((2, 4, 4)),
            DMA((2, 4, 4)),
            DMA((NX, NZ)),
            DMA((NX, NZ)),
            DMA((NX,)),
            DMA((NX,)),
            DMA((NX,)),
            DMA((NX,)),
            DMA((2, 4)),
            DMA((2, 4)),
            DMA((NZ,)),
            DMA((NZ,)),
        ],
        aug, ints, wcol, labels,
    )
    grad_share = lax.psum_scatter(label_grad, "dp", scatter_dimension=1, tiled=True).astype(F32)
    label_step = grad_share * lax.rsqrt(
        jnp.mean(grad_share * grad_share, axis=2, keepdims=True) + epsilon
    )
    query_grad, knowledge_grad = run(
        grads_kernel,
        3,
        [((Q, D), F32), ((8, 8, D), F32)],
        [
            pltpu.VMEM((PAIRS, 4 * Q, 128), BF16),
            pltpu.VMEM((PAIRS, 128, 2 * Q), F32),
            pltpu.VMEM((PAIRS, 1, 2 * Q), F32),
            pltpu.VMEM((NZ, NX, 2, 32, D), BF16),
            pltpu.VMEM((8, NZ, 32, D), BF16),
            pltpu.VMEM((NZ, NY, 4, 16, D), BF16),
            pltpu.VMEM((NY, NZ, 4, 16, D), BF16),
            pltpu.VMEM((NZ, 4, 16, D), BF16),
            pltpu.VMEM((NZ, 4, 16, D), BF16),
            DMA((8, NZ)),
            DMA((8, NZ)),
            DMA((NY, NZ)),
            DMA((NY, NZ)),
            DMA((NZ,)),
            DMA((NZ,)),
        ],
        asks, keys, queries, d_aug, out_proj, mixed_t, total, tile_weight,
        in_specs=[S] + [V] * 7,
    )
    return (loss[0], query_grad, knowledge_grad, label_step)


def solution(mesh):
    placed = (
        P(("dp", "table"), None),
        P(("dp", "table"), None),
        P("table", None, None),
        P(),
        P("table", None, None),
        P(("dp", "table"), None),
        P(("dp", "table"), None),
    )
    return jax.shard_map(
        on_device,
        mesh=mesh,
        in_specs=placed,
        out_specs=(
            P(("dp", "table")),
            P(("dp", "table"), None),
            P("table", "dp", None),
            P("table", "dp", None),
        ),
        check_vma=False,
    )
```

time: 465 us -> 242 us (0.52)
  the two profiles are of different devices: /device:TPU:16 before, /device:TPU:33 now
where the time goes in v1:
time: 242 us; the launch traced here: 241 us
  Pallas kernels  211 us (87%)
  between operations  14.3 us (6%)
  other arithmetic  11.5 us (5%)
  local copies, waits for them, and re-layouts  4.63 us (2%)
    pallas_call x3, Pallas kernels, run(): pl.pallas_call(kernel, out_shape=[jax.ShapeDtypeStruct(shape, dtype) for...  211 us
    reduce_sum x1, other arithmetic, prepare(): slot_query = Q + jnp.sum(jnp.where(held, query - Q, 0), axis=2)  5.47 us
  transfers between devices with their start and end apart: 1, of which 0 were waited for; matrix products, arithmetic and copies ran while one was open for 0% of the time, Pallas kernels for 34%

profile of v1, /device:TPU:33, one launch (start us, length us, event | category | flops | bytes accessed | tf_op | source)
XLA Modules:
  0.0 241.2 jit_solution(12573238070300461838)
XLA Ops:
  7.2 0.8 add_select_fusion.1
  8.0 0.7 fusion.8
  8.7 0.7 select_reduce_fusion.6
  9.5 0.1 fusion
  9.6 5.5 %select_reduce_fusion = (s32[64,16]{1,0:T(8,128)S(1)}, s32[64,16]{1,0:T(8,128)S(1)}, s32[64,16]{1,0:T(8,128)S(1)}, s32[64,16]{1,0:T(8,128)S(1)}, s32[64,16]{1,0:T(8,128)S(1)}) fusion(s32[128]{0:T(128)S(1)} %iota_add_fusion, s32[64,128]{1,0:T(8,128)S(1)} %fusion, s32[128]{0:T(128)S(1)} %get-tuple-element.36, pred[64,128]{1,0:T(8,128)(4,1)S(1)} %get-tuple-element.43, ...), kind=kLoop, calls=%fused_computation.2 | loop fusion | flops 1960960 | bytes 88576 | tf_op jit(solution)/shard_map/reduce_sum | solution.py:591
  15.2 0.7 add_select_fusion.3
  15.9 0.1 select_reduce_fusion.5
  16.1 0.1 reshape.209
  16.2 0.1 sub.43
  16.3 0.1 sub.41
  16.4 0.1 sub.39
  16.8 0.1 concatenate.6
  16.9 0.1 fusion.7.msg
  17.1 1.1 copy-done.1
  18.2 58.3 %shard_map.102 = (bf16[32,64,768]{2,1,0:T(8,128)(2,1)}, bf16[128,768]{1,0:T(8,128)(2,1)S(1)}, f32[6,128,128]{2,1,0:T(8,128)S(1)}, f32[6,1,256]{2,1,0:T(1,128)S(1...) custom-call(bf16[8,64,768]{2,1,0:T(8,128)(2,1)S(1)} %copy-done.1, s32[8,128]{1,0:T(8,128)S(1)} %pad.12.wanted, ...), custom_call_target="tpu_custom_call" | custom-call | flops 4000000000 | bytes 40000000 | tf_op jit(solution)/shard_map/pallas_call | solution.py:561
  76.5 0.1 reshape.211
  76.7 0.5 copy.25
  77.2 70.9 %shard_map.103 = (f32[128,768]{1,0:T(8,128)S(1)}, f32[1,128]{1,0:T(1,128)S(1)}, bf16[2,512,768]{2,1,0:T(8,128)(2,1)}) custom-call(bf16[128,768]{1,0:T(8,128)(2,1)S(1)} %get-tuple-element.15.aug, s32[8,4,8,128]{3,2,1,0:T(8,128)S(1)} %get-tuple-element.16.ints, s32[8,128,8]{2,1,0:T(8,128)S(1)} %pad.14.wcol, bf16[2,512,768]{2,1,0:T(8,128)(2,1)} %labels.1), custom_call_target="tpu_custom_call" | custom-call | flops 4000000000 | bytes 40000000 | tf_op jit(solution)/shard_map/pallas_call | solution.py:561
  148.1 81.4 %shard_map.104 = (f32[128,768]{1,0:T(8,128)S(1)}, f32[8,8,768]{2,1,0:T(8,128)S(1)}) custom-call(s32[8,8,128]{2,1,0:T(8,128)S(1)} %get-tuple-element.18.asks, bf16[32,64,768]{2,1,0:T(8,128)(2,1)} %get-tuple-element.19.keys, bf16[128,768]{1,0:T(8,128)(2,1)S(1)} %copy-done.2, f32[128,768]{1,0:T(8,128)S(1)} %get-tuple-element.20.d_aug, ...), custom_call_target="tpu_custom_call" | custom-call | flops 4000000000 | bytes 40000000 | tf_op jit(solution)/shard_map/pallas_call | solution.py:561
  229.6 1.0 fusion.5
  230.7 1.8 convert_multiply_fusion
  232.4 0.5 copy.29
  232.9 0.7 copy.30
  233.7 0.7 copy.31
  (35 shorter events, 0.7 us)
Async XLA Ops:
  7.2 9.9 %copy-start = (bf16[768,768]{1,0:T(8,128)(2,1)S(1)}, bf16[768,768]{1,0:T(8,128)(2,1)}, u32[]{:S(2)}) copy-start(bf16[768,768]{1,0:T(8,128)(2,1)} %out_proj.3) | copy-start | bytes 3538948
  7.2 9.9 %copy-start.2 = (bf16[128,768]{1,0:T(8,128)(2,1)S(1)}, bf16[128,768]{1,0:T(8,128)(2,1)}, u32[]{:S(2)}) copy-start(bf16[128,768]{1,0:T(8,128)(2,1)} %queries.3) | copy-start | bytes 589828
  7.2 222.4 %reduce-scatter.2.cloned.1.call-start = ((), (), s32[]{:S(2)}) async-start(), calls=%async_computation.1 | async-start | bytes 1769472 | tf_op jit(solution)/shard_map/reduce_scatter | solution.py:687
  17.0 1.1 copy-start.1
Sparse Core Ops, SparseCore 0:
  148.3 43.8 reduce-scatter.1

commit v2 on v1

--- a/solution.py
+++ b/solution.py
@@ -218,16 +218,19 @@
 
 def labels_kernel(
     aug, ints, wcol, labels,
-    d_aug, loss, label_grad,
+    d_aug, loss, label_step,
     rows, served, got, back, back_got, lstage, lgot, dlogit, onehot, lpart, lsend, lrecv,
-    psend, prbuf,
+    psend, prbuf, label_grad, label_got,
     z_send, z_recv, x_send, x_recv, b_send, b_recv, s_send, s_recv, p_send, p_recv, q_send, q_recv,
+    g_send, g_recv,
 ):
     y, c, z, x = where_am_i()
+    dp = y * 2 + c
     right, left = dev(y, c, (z + 1) % NZ, x), dev(y, c, (z + NZ - 1) % NZ, x)
     greet(
         [dev(y, c, z, (x + dx) % NX) for dx in range(1, NX)]
         + [dev(y, c, (z + d) % NZ, x) for d in range(1, NZ)]
+        + [((dp + d) % 8, z * NX + x) for d in range(1, 8)]
     )
     ring = {}
 
@@ -258,37 +261,30 @@
     def serve(zs):
         picked = tn(onehot[zs], rows[zs]).astype(BF16)
         served[zs] = picked.reshape(NX, 2, 16, D)
-        got[x, :, zs] = served[zs, x]
+        got[zs, :, x] = served[zs, x]
         for dx in range(1, NX):
             px = (x + dx) % NX
             cp = remote(
-                served.at[zs, px], got.at[x, :, zs], x_send.at[dx, zs], x_recv.at[dx, zs],
+                served.at[zs, px], got.at[zs, :, x], x_send.at[dx, zs], x_recv.at[dx, zs],
                 dev(y, c, z, px),
             )
             cp.start()
             sent.append(cp)
 
-    serve(z)
-    for step in range(1, 4):
-        for k in range(4):
-            for way in (0, 1):
-                ring[way, step - 1, k].wait_recv()
-                if step < 3 or (k < 2) == (way == 0):
-                    ring_send(way, step, k)
-        serve((z + NZ - step) % NZ)
-        serve((z + step) % NZ)
-    for k in range(4):
-        ring[0 if k < 2 else 1, 3, k].wait_recv()
-    serve((z + 4) % NZ)
-    label = lax.broadcasted_iota(jnp.int32, (128, 512), 1)
-    lane = lax.broadcasted_iota(jnp.int32, (NZ, 16, 128), 2)
-    source = lax.broadcasted_iota(jnp.int32, (NZ, 16, 128), 0)
-
-    def work(xs):
+    label = lax.broadcasted_iota(jnp.int32, (64, 512), 1)
+    lane = lax.broadcasted_iota(jnp.int32, (NX, 16, 128), 2)
+    lstage[...] = jnp.zeros_like(lstage)
+
+    def work(zs):
+        for dx in range(1, NX):
+            remote(
+                served.at[0, 0], got.at[zs, :, 0], x_send.at[dx, zs], x_recv.at[dx, zs], right
+            ).wait_recv()
+
         def cluster(cl, carry):
-            entries = got[xs, cl].reshape(128, D)
+            entries = got[zs, cl].reshape(64, D)
             logits = nt(entries, labels[cl])
-            want = wcol[xs * 2 + cl]
+            want = wcol[zs * 2 + cl]
             live = (want[:, 4:5] > 0).astype(F32)
             hit = label == want[:, 0:1]
             for j in range(1, 4):
@@ -299,60 +295,111 @@
             inv = 1.0 / (1.0 + e)
             sig = jnp.where(logits >= 0, inv, 1.0 - inv)
             dl = ((sig - jnp.where(hit, 1.0, 0.0)) * live).astype(BF16)
-            dlogit[cl, xs] = dl
-            back[xs, cl] = nn(dl, labels[cl]).astype(BF16).reshape(NZ, 16, D)
-            spread = jnp.broadcast_to(pair_loss, (128, 128)).reshape(NZ, 16, 128)
-            lstage[xs, cl] = jnp.sum(jnp.where(lane == source, spread, 0.0), axis=0)
+            dlogit[zs, cl] = dl
+            back[zs, cl] = nn(dl, labels[cl]).astype(BF16).reshape(NX, 16, D)
+            spread = jnp.broadcast_to(pair_loss, (64, 128)).reshape(NX, 16, 128)
+            lstage[:, cl] = jnp.where(lane == zs, spread, lstage[:, cl])
             return carry
 
         lax.fori_loop(0, 2, cluster, 0)
 
-    back_copies = []
-    for dx in (0, 1, 3, 2):
-        xs = (x + NX - dx) % NX
-        if dx:
-            for zs in range(NZ):
-                remote(
-                    served.at[0, 0], got.at[xs, :, 0], x_send.at[dx, zs], x_recv.at[dx, zs], right
-                ).wait_recv()
-        work(xs)
-        if dx == 0:
-            back_got[x] = back[x]
-            lgot[x] = lstage[x]
-        else:
-            to = dev(y, c, z, xs)
-            for cp in (
-                remote(back.at[xs], back_got.at[x], b_send.at[dx], b_recv.at[dx], to),
-                remote(lstage.at[xs], lgot.at[x], s_send.at[dx], s_recv.at[dx], to),
-            ):
-                cp.start()
-                back_copies.append(cp)
-    for cl in range(2):
-        label_grad[cl] = tn(
-            dlogit[cl].reshape(512, 512), got[:, cl].reshape(512, D)
-        ).astype(BF16)
-    for cp in back_copies:
-        cp.wait()
+    def send_back(zs):
+        back_got[zs, x] = back[zs, :, x]
+        for dx in range(1, NX):
+            px = (x + dx) % NX
+            cp = remote(
+                back.at[zs, :, px], back_got.at[zs, x], b_send.at[dx, zs], b_recv.at[dx, zs],
+                dev(y, c, z, px),
+            )
+            cp.start()
+            sent.append(cp)
+
+    serve(z)
+    pending = [z]
+    for step in range(1, 4):
+        for k in range(4):
+            for way in (0, 1):
+                ring[way, step - 1, k].wait_recv()
+                if step < 3 or (k < 2) == (way == 0):
+                    ring_send(way, step, k)
+        fresh = [(z + NZ - step) % NZ, (z + step) % NZ]
+        for zs in fresh:
+            serve(zs)
+        for zs in pending:
+            work(zs)
+        pending = fresh
+    for k in range(4):
+        ring[0 if k < 2 else 1, 3, k].wait_recv()
+    serve((z + 4) % NZ)
+    for zs in pending:
+        work(zs)
+        send_back(zs)
+    work((z + 4) % NZ)
+    for d in (4, 2, 6, 1, 7, 0):
+        send_back((z + d) % NZ)
+    loss_copies = []
+    for dx in range(1, NX):
+        px = (x + dx) % NX
+        cp = remote(lstage.at[px], lgot.at[x], s_send.at[dx], s_recv.at[dx], dev(y, c, z, px))
+        cp.start()
+        loss_copies.append(cp)
+    lgot[x] = lstage[x]
 
     def partial(zs):
-        pairs = back_got[:, :, zs].reshape(128, D)
-        return nn(onehot[zs], pairs)
-
-    p_copies = []
-
-    def chain_send(way, step, value, dest_rows):
-        psend[way, step, dest_rows] = value.astype(BF16)
+        for dx in range(1, NX):
+            remote(
+                back.at[0, :, 0], back_got.at[zs, 0], b_send.at[dx, zs], b_recv.at[dx, zs], right
+            ).wait_recv()
+        return nn(onehot[zs], back_got[zs].reshape(128, D))
+
+    label_copies = []
+
+    def label_part(cl):
+        entries = got[:, cl].reshape(512, D)
+        for part in range(2):
+            columns = slice(part * 256, part * 256 + 256)
+            value = tn(dlogit[:, cl, :, columns].reshape(512, 256), entries)
+            label_grad[cl, part * 4 : part * 4 + 4] = value.astype(BF16).reshape(4, 64, D)
+        label_got[cl, dp] = label_grad[cl, dp]
+        for d in range(1, 8):
+            to = (dp + d) % 8
+            cp = remote(
+                label_grad.at[cl, to], label_got.at[cl, dp], g_send.at[cl, d], g_recv.at[cl, d],
+                (to, z * NX + x),
+            )
+            cp.start()
+            label_copies.append(cp)
+
+    p_copies = {}
+
+    def chain_send(way, step, h, value):
+        piece = pl.ds(h * 64, 64)
+        psend[way, step, piece] = value.astype(BF16)
         cp = remote(
-            psend.at[way, step, dest_rows], prbuf.at[way, step, dest_rows],
-            p_send.at[way, step], p_recv.at[way, step], right if way == 0 else left,
+            psend.at[way, step, piece], prbuf.at[way, step, piece],
+            p_send.at[way, step, h], p_recv.at[way, step, h], right if way == 0 else left,
         )
         cp.start()
-        p_copies.append(cp)
-        return cp
-
-    low, high, whole = pl.ds(0, 64), pl.ds(64, 64), pl.ds(0, Q)
+        p_copies[way, step, h] = cp
+
+    label_part(0)
     far = partial((z + 4) % NZ)
-    previous = [chain_send(0, 0, far[:64], low), chain_send(1, 0, far[64:], high)]
+    for way in (0, 1):
+        chain_send(way, 0, way, far[way * 64 : way * 64 + 64])
+    label_part(1)
+    for step in range(1, 4):
+        d = 4 - step
+        own = [partial((z + d) % NZ), partial((z + NZ - d) % NZ)]
+        for h in (0, 1):
+            for way in (h, 1 - h):
+                value = own[way][h * 64 : h * 64 + 64]
+                if (way, step - 1, h) in p_copies:
+                    p_copies[way, step - 1, h].wait_recv()
+                    value = value + prbuf[way, step - 1, h * 64 : h * 64 + 64].astype(F32)
+                chain_send(way, step, h, value)
+    mine = partial(z)
+    for cp in loss_copies:
+        cp.wait()
     losses = jnp.concatenate([lgot[i].reshape(32, 128) for i in range(NX)], axis=0).astype(BF16)
     out_lane = lax.broadcasted_iota(jnp.int32, (Q, 128), 1)
     lpart[...] = jnp.zeros_like(lpart)
@@ -370,29 +417,22 @@
         cp.start()
         l_copies.append(cp)
     lrecv[z] = lsend[...]
-    for step in range(1, 4):
-        d = 4 - step
-        to_right, to_left = partial((z + d) % NZ), partial((z + NZ - d) % NZ)
-        for cp in previous:
-            cp.wait_recv()
-        if step == 1:
-            zeros = jnp.zeros((64, D), F32)
-            in_right = jnp.concatenate([prbuf[0, 0, :64].astype(F32), zeros], axis=0)
-            in_left = jnp.concatenate([zeros, prbuf[1, 0, 64:].astype(F32)], axis=0)
-        else:
-            in_right, in_left = prbuf[0, step - 1].astype(F32), prbuf[1, step - 1].astype(F32)
-        previous = [
-            chain_send(0, step, to_right + in_right, whole),
-            chain_send(1, step, to_left + in_left, whole),
-        ]
-    mine = partial(z)
-    for cp in previous:
-        cp.wait_recv()
+    for h in (0, 1):
+        for way in (0, 1):
+            p_copies[way, 3, h].wait_recv()
     d_aug[...] = mine + prbuf[0, 3].astype(F32) + prbuf[1, 3].astype(F32)
     for cp in l_copies:
         cp.wait()
     loss[...] = jnp.sum(lrecv[:, pl.ds(z, 1), :], axis=0) * (1.0 / 2048.0)
-    for cp in p_copies:
+    for cp in label_copies:
+        cp.wait()
+    for cl in range(2):
+        grad = label_got[cl, 0].astype(F32)
+        for i in range(1, 8):
+            grad = grad + label_got[cl, i].astype(F32)
+        square = jnp.mean(grad * grad, axis=1, keepdims=True)
+        label_step[cl] = grad * lax.rsqrt(square + epsilon)
+    for cp in p_copies.values():
         cp.wait_send()
     for cp in ring.values():
         cp.wait_send()
@@ -515,17 +555,17 @@
         def _():
             compute((z + offset(i)) % NZ)
 
-        @pl.when((i >= 1) & (i < 9))
+        @pl.when((i >= 3) & (i < 11))
         def _():
-            gather_tiles((z + offset(i - 1)) % NZ)
-
-        @pl.when(i >= 2)
+            gather_tiles((z + offset(i - 3)) % NZ)
+
+        @pl.when(i >= 5)
         def _():
-            gather_shards((z + offset(i - 2)) % NZ, offset(i - 2))
+            gather_shards((z + offset(i - 5)) % NZ, offset(i - 5))
 
         return carry
 
-    lax.fori_loop(0, 10, body, 0)
+    lax.fori_loop(0, 13, body, 0)
     d_query = jnp.concatenate([unstack_heads(d_acc[p]).T for p in range(PAIRS)], axis=1)
     query_grad[...] = d_rows + d_query
     for d in range(1, NZ):
@@ -648,45 +688,45 @@
         ],
         knowledge, wanted, queries, tile_weight, out_proj, msg,
     )
-    wcol = ints[:, :, :5, :32].reshape(NZ, NX, 5, 2, 16).transpose(1, 3, 0, 4, 2)
-    wcol = jnp.pad(wcol.reshape(8, 128, 5), ((0, 0), (0, 0), (0, 3)))
-    d_aug, loss, label_grad = run(
+    wcol = ints[:, :, :5, :32].reshape(NZ, NX, 5, 2, 16).transpose(0, 3, 1, 4, 2)
+    wcol = jnp.pad(wcol.reshape(16, 64, 5), ((0, 0), (0, 0), (0, 3)))
+    d_aug, loss, label_step = run(
         labels_kernel,
         2,
-        [((Q, D), F32), ((1, Q), F32), ((2, 512, D), BF16)],
+        [((Q, D), F32), ((1, Q), F32), ((2, 64, D), F32)],
         [
             pltpu.VMEM((NZ, Q, D), BF16),
             pltpu.VMEM((NZ, NX, 2, 16, D), BF16),
-            pltpu.VMEM((NX, 2, NZ, 16, D), BF16),
-            pltpu.VMEM((NX, 2, NZ, 16, D), BF16),
-            pltpu.VMEM((NX, 2, NZ, 16, D), BF16),
+            pltpu.VMEM((NZ, 2, NX, 16, D), BF16),
+            pltpu.VMEM((NZ, 2, NX, 16, D), BF16),
+            pltpu.VMEM((NZ, NX, 2, 16, D), BF16),
             pltpu.VMEM((NX, 2, 16, 128), F32),
             pltpu.VMEM((NX, 2, 16, 128), F32),
-            pltpu.VMEM((2, NX, 128, 512), BF16),
+            pltpu.VMEM((NZ, 2, 64, 512), BF16),
             pltpu.VMEM((NZ, Q, 128), BF16),
             pltpu.VMEM((Q, 128), F32),
             pltpu.VMEM((NZ, 128), F32),
             pltpu.VMEM((NZ, NZ, 128), F32),
             pltpu.VMEM((2, 4, Q, D), BF16),
             pltpu.VMEM((2, 4, Q, D), BF16),
+            pltpu.VMEM((2, 8, 64, D), BF16),
+            pltpu.VMEM((2, 8, 64, D), BF16),
             DMA((2, 4, 4)),
             DMA((2, 4, 4)),
             DMA((NX, NZ)),
             DMA((NX, NZ)),
+            DMA((NX, NZ)),
+            DMA((NX, NZ)),
             DMA((NX,)),
             DMA((NX,)),
-            DMA((NX,)),
-            DMA((NX,)),
-            DMA((2, 4)),
-            DMA((2, 4)),
+            DMA((2, 4, 2)),
+            DMA((2, 4, 2)),
             DMA((NZ,)),
             DMA((NZ,)),
+            DMA((2, 8)),
+            DMA((2, 8)),
         ],
         aug, ints, wcol, labels,
-    )
-    grad_share = lax.psum_scatter(label_grad, "dp", scatter_dimension=1, tiled=True).astype(F32)
-    label_step = grad_share * lax.rsqrt(
-        jnp.mean(grad_share * grad_share, axis=2, keepdims=True) + epsilon
     )
     query_grad, knowledge_grad = run(
         grads_kernel,

time: 242 us -> 202 us (0.83)
  the two profiles are of different devices: /device:TPU:33 before, /device:TPU:16 now
where the time goes in v2:
time: 202 us; the launch traced here: 200 us
  Pallas kernels  178 us (88%)
  local copies, waits for them, and re-layouts  11.9 us (6%)
  other arithmetic  8.64 us (4%)
    pallas_call x3, Pallas kernels, run(): pl.pallas_call(kernel, out_shape=[jax.ShapeDtypeStruct(shape, dtype) for...  178 us
    reduce_sum x1, other arithmetic, prepare(): slot_query = Q + jnp.sum(jnp.where(held, query - Q, 0), axis=2)  5.47 us
    unnamed x16, local copies, waits for them, and re-layouts  5.41 us

profile of v2, /device:TPU:16, one launch (start us, length us, event | category | flops | bytes accessed | tf_op | source)
XLA Modules:
  0.0 199.7 jit_solution(5375957160741611225)
XLA Ops:
  0.7 0.8 add_select_fusion.3
  1.5 0.1 select_reduce_fusion.5
  1.6 0.1 reshape.201
  1.7 0.7 add_select_fusion.1
  2.4 0.7 select_reduce_fusion.6
  3.2 0.7 fusion.7
  3.9 0.1 fusion
  4.1 5.5 %select_reduce_fusion = (s32[64,16]{1,0:T(8,128)S(1)}, s32[64,16]{1,0:T(8,128)S(1)}, s32[64,16]{1,0:T(8,128)S(1)}, s32[64,16]{1,0:T(8,128)S(1)}, s32[64,16]{1,0:T(8,128)S(1)}) fusion(s32[128]{0:T(128)S(1)} %iota_add_fusion, s32[64,128]{1,0:T(8,128)S(1)} %fusion, s32[128]{0:T(128)S(1)} %get-tuple-element.36, pred[64,128]{1,0:T(8,128)(4,1)S(1)} %get-tuple-element.43, ...), kind=kLoop, calls=%fused_computation.2 | loop fusion | flops 1960960 | bytes 88576 | tf_op jit(solution)/shard_map/reduce_sum | solution.py:631
  10.2 0.1 concatenate.6
  10.4 0.1 fusion.6.msg
  10.5 1.1 copy-done.2
  11.6 58.7 %shard_map.102 = (bf16[32,64,768]{2,1,0:T(8,128)(2,1)}, bf16[128,768]{1,0:T(8,128)(2,1)S(1)}, f32[6,128,128]{2,1,0:T(8,128)S(1)}, f32[6,1,256]{2,1,0:T(1,128)S(1...) custom-call(bf16[8,64,768]{2,1,0:T(8,128)(2,1)S(1)} %copy-done.2, s32[8,128]{1,0:T(8,128)S(1)} %pad.12.wanted, ...), custom_call_target="tpu_custom_call" | custom-call | flops 4000000000 | bytes 40000000 | tf_op jit(solution)/shard_map/pallas_call | solution.py:601
  70.3 0.7 copy-done.4
  71.0 0.7 copy.24
  71.7 1.7 reshape.203
  73.4 2.1 %copy.25 = s32[8,2,4,16,5]{4,3,2,1,0:T(8,128)} copy(s32[8,2,4,16,5]{3,1,0,4,2:T(2,128)} %bitcast.78) | data formatting | bytes 40960 | tf_op jit(solution)/shard_map/transpose | solution.py:691
  75.5 1.1 pad.14.wcol
  76.6 0.9 copy-done.5
  77.5 59.9 %shard_map.103 = (f32[128,768]{1,0:T(8,128)S(1)}, f32[1,128]{1,0:T(1,128)S(1)}, f32[2,64,768]{2,1,0:T(8,128)S(1)}) custom-call(bf16[128,768]{1,0:T(8,128)(2,1)S(1)} %copy-done.5, s32[8,4,8,128]{3,2,1,0:T(8,128)S(1)} %get-tuple-element.16.ints, s32[16,64,8]{2,1,0:T(8,128)S(1)} %pad.14.wcol, bf16[2,512,768]{2,1,0:T(8,128)(2,1)S(1)} %copy-done), custom_call_target="tpu_custom_call" | custom-call | flops 4000000000 | bytes 40000000 | tf_op jit(solution)/shard_map/pallas_call | solution.py:601
  137.5 59.5 %shard_map.104 = (f32[128,768]{1,0:T(8,128)S(1)}, f32[8,8,768]{2,1,0:T(8,128)S(1)}) custom-call(s32[8,8,128]{2,1,0:T(8,128)S(1)} %get-tuple-element.18.asks, bf16[32,64,768]{2,1,0:T(8,128)(2,1)} %get-tuple-element.19.keys, bf16[128,768]{1,0:T(8,128)(2,1)S(1)} %copy-done.3, f32[128,768]{1,0:T(8,128)S(1)} %get-tuple-element.20.d_aug, ...), custom_call_target="tpu_custom_call" | custom-call | flops 4000000000 | bytes 40000000 | tf_op jit(solution)/shard_map/pallas_call | solution.py:601
  197.0 0.5 copy.30
  197.5 0.7 copy.31
  198.3 0.7 copy.32
  198.9 0.7 copy.33
  (36 shorter events, 0.8 us)
Async XLA Ops:
  0.6 9.8 %copy-start.1 = (bf16[768,768]{1,0:T(8,128)(2,1)S(1)}, bf16[768,768]{1,0:T(8,128)(2,1)}, u32[]{:S(2)}) copy-start(bf16[768,768]{1,0:T(8,128)(2,1)} %out_proj.3) | copy-start | bytes 3538948
  0.6 9.8 %copy-start.3 = (bf16[128,768]{1,0:T(8,128)(2,1)S(1)}, bf16[128,768]{1,0:T(8,128)(2,1)}, u32[]{:S(2)}) copy-start(bf16[128,768]{1,0:T(8,128)(2,1)} %queries.3) | copy-start | bytes 589828
  10.5 1.1 copy-start.2
  70.3 0.7 copy-start.4
  71.0 5.6 %copy-start = (bf16[2,512,768]{2,1,0:T(8,128)(2,1)S(1)}, bf16[2,512,768]{2,1,0:T(8,128)(2,1)}, u32[]{:S(2)}) copy-start(bf16[2,512,768]{2,1,0:T(8,128)(2,1)} %labels.1) | copy-start | bytes 4718596
  76.6 0.9 copy-start.5

commit v3 on v2

--- a/solution.py
+++ b/solution.py
@@ -1,6 +1,3 @@
-import functools
-import math
-
 import jax
 import jax.numpy as jnp
 from jax import lax
@@ -12,7 +9,6 @@
 DMA = pltpu.SemaphoreType.DMA
 F32 = jnp.float32
 BF16 = jnp.bfloat16
-HEADS = 12
 PAIRS = 6
 Q = 128
 D = 768
@@ -21,7 +17,7 @@
 NY = 4
 epsilon = 1e-06
 LOG2E = 1.4426950408889634
-VMEM_LIMIT = 50 << 20
+VMEM_LIMIT = 56 << 20
 
 
 def where_am_i():
@@ -79,26 +75,22 @@
 
 
 def keys_kernel(
-    know, wanted, queries, tile_weight, out_proj, msg,
-    keys, aug, mixed_t, total, asks, ints,
-    half, r0, r1, r2, l0, l1, l2, far, stage, stacked, acc, mid,
-    ask_smem, z_send, z_recv, x_send, x_recv, a_send, a_recv, m_send, m_recv, n_send, n_recv, l_sem,
+    know, numbers, queries, out_proj,
+    keys, aug, mixed_t, total, tile_weight, onehot, facts, ask_smem,
+    wanted, asks, half, r0, r1, r2, l0, l1, l2, far, stage, stacked, acc, note, noted, fact,
+    z_send, z_recv, x_send, x_recv, a_send, a_recv, m_send, m_recv, n_send, n_recv, l_sem,
 ):
     y, c, z, x = where_am_i()
+    dp = y * 2 + c
     me = x * 2 + c
     right, left = dev(y, c, (z + 1) % NZ, x), dev(y, c, (z + NZ - 1) % NZ, x)
     group = [((x + dx) % NX, (c + dc) % 2) for dx, dc in XC]
     greet(
         [dev(y, pc, z, px) for px, pc in group[1:]]
         + [dev(y, c, (z + d) % NZ, x) for d in range(1, NZ)]
+        + [((dp + d) % 8, z * NX + x) for d in range(1, 8)]
     )
     half[...] = know[:, pl.ds(pl.multiple_of(c * 32, 32), 32), :]
-    ask_copies = []
-    for j in range(1, 8):
-        px, pc = group[j]
-        cp = remote(wanted, asks.at[me], a_send.at[j], a_recv.at[j], dev(y, pc, z, px))
-        cp.start()
-        ask_copies.append(cp)
     ring = {}
     slots = ((half, r0, r1, r2, far), (half, l0, l1, l2, far))
 
@@ -114,14 +106,80 @@
     for k in range(4):
         for way in (0, 1):
             ring_send(way, 0, k)
-    m_copies = []
-    for dx in range(1, NX):
-        px = (x + dx) % NX
-        cp = remote(msg.at[px], mid.at[x], m_send.at[dx], m_recv.at[dx], dev(y, c, z, px))
+    owner = lax.broadcasted_iota(jnp.int32, (32, Q), 0)
+    weight, tile = jnp.zeros((32, Q), F32), jnp.zeros((32, Q), jnp.int32)
+    for r in range(4):
+        named = numbers[r : r + 1, :]
+        hit = (named >> 3) == owner
+        weight = weight + jnp.where(hit, 1.0, 0.0)
+        tile = jnp.maximum(tile, jnp.where(hit, named & 7, 0))
+    wanted[...] = jnp.broadcast_to(jnp.max(tile, axis=1, keepdims=True), (32, 128))
+    ask_copies = []
+    for j in range(1, 8):
+        px, pc = group[j]
+        cp = remote(wanted, asks.at[me], a_send.at[j], a_recv.at[j], dev(y, pc, z, px))
         cp.start()
-        m_copies.append(cp)
+        ask_copies.append(cp)
     asks[me] = wanted[...]
-    mid[x] = msg[x]
+    for zo in range(NZ):
+        tile_weight[zo, 0:NX] = weight[zo * NX : zo * NX + NX]
+    cluster = lax.broadcasted_iota(jnp.int32, (64, Q), 0)
+    ids = [numbers[4 + i : 5 + i, :] for i in range(4)]
+    member = ids[0] == cluster
+    for i in range(1, 4):
+        member = member | (ids[i] == cluster)
+    row = lax.broadcasted_iota(jnp.int32, (Q, 128), 0)
+    lane = lax.broadcasted_iota(jnp.int32, (Q, 128), 1)
+    before = jnp.where(row < lane, 1.0, 0.0).astype(BF16)
+    rank = nn(jnp.where(member, 1.0, 0.0).astype(BF16), before)
+    rank = jnp.where(member, rank, -1.0)
+    picks = [numbers[8 + j : 9 + j, :] for j in range(4)]
+    columns = []
+    for j in range(4):
+        column = picks[j] >> 9
+        named = jnp.where(column == 0, ids[0], 0)
+        for i in range(1, 4):
+            named = jnp.where(column == i, ids[i], named)
+        columns.append(named)
+    columns += [(pick & 511) >> 8 for pick in picks] + [pick & 255 for pick in picks]
+    columns += [jnp.ones_like(picks[0])] + [jnp.zeros_like(picks[0])] * 3
+    columns = jnp.concatenate(columns, axis=0).astype(F32)
+    for i in range(NZ):
+        note[i, 0:8] = rank[i * 8 : i * 8 + 8]
+        note[i, 8:24] = columns
+    note_copies = []
+    for d in range(1, NZ):
+        zp = (z + d) % NZ
+        cp = remote(
+            note.at[zp], noted.at[NZ - d], m_send.at[d], m_recv.at[NZ - d], dev(y, c, zp, x)
+        )
+        cp.start()
+        note_copies.append(cp)
+    noted[0] = note[z]
+
+    def slots_and_facts():
+        for d in range(1, NZ):
+            remote(note.at[0], noted.at[d], m_send.at[d], m_recv.at[d], right).wait_recv()
+        spread = jnp.where(
+            lax.broadcasted_iota(jnp.int32, (16, 128), 0)
+            == lax.broadcasted_iota(jnp.int32, (16, 128), 1) // 16,
+            1.0, 0.0,
+        ).astype(BF16)
+        place = (lane % 16).astype(F32)
+        about = noted[:, 8:24, :].reshape(128, Q).T
+        value = jnp.zeros((128, 128), F32)
+        for o in range(NZ):
+            hot = jnp.where(tn(noted[o, 0:16].astype(BF16), spread) == place, 1.0, 0.0).astype(BF16)
+            onehot[o] = hot
+            value = value + tn(hot, jnp.where(lane // 16 == o, about, 0.0).astype(BF16))
+        fact[...] = value.reshape(NX, 2, 16, 128)
+        facts[x] = fact[x]
+        for dx in range(1, NX):
+            px = (x + dx) % NX
+            cp = remote(fact.at[px], facts.at[x], n_send.at[dx], n_recv.at[dx], dev(y, c, z, px))
+            cp.start()
+            note_copies.append(cp)
+
     stack_heads(queries[...], stacked)
     acc[...] = jnp.zeros_like(acc)
     total[...] = jnp.zeros_like(total)
@@ -135,7 +193,7 @@
     def serve(zo, shard):
         row = pl.ds(pl.multiple_of(c * 32, 32), 32)
         for j, (px, pc) in enumerate(group):
-            tile = ask_smem[px * 2 + pc, zo, x]
+            tile = jnp.clip(ask_smem[px * 2 + pc, zo * NX + x, 0], 0, 7)
             if j == 0:
                 keys[zo * NX + x, row] = shard[tile]
                 continue
@@ -155,7 +213,7 @@
             ).wait_recv()
 
     def attend(zo):
-        w = weight_block(tile_weight[zo])
+        w = weight_block(tile_weight[zo, 0:NX])
 
         def pair(p, carry):
             lanes = pl.ds(pl.multiple_of(p * 128, 128), 128)
@@ -172,17 +230,6 @@
         ring[way, step, k].wait_recv()
 
     serve(z, half)
-    for cp in m_copies:
-        cp.wait()
-    n_copies = []
-    for d in range(1, NZ):
-        zp = (z + d) % NZ
-        cp = remote(
-            mid.at[:, zp], ints.at[z], n_send.at[d], n_recv.at[d], dev(y, c, zp, x)
-        )
-        cp.start()
-        n_copies.append(cp)
-    ints[z] = mid[:, z]
     pending = [z]
     for step in range(1, 4):
         for k in range(4):
@@ -195,6 +242,8 @@
         for zo in pending:
             arrived(zo)
             attend(zo)
+        if step == 1:
+            slots_and_facts()
         pending = [(z + NZ - step) % NZ, (z + step) % NZ]
     for k in range(4):
         wait_step(0 if k < 2 else 1, 3, k)
@@ -202,24 +251,19 @@
     for zo in pending:
         arrived(zo)
         attend(zo)
-    for cp in n_copies:
-        cp.wait()
     arrived((z + 4) % NZ)
     attend((z + 4) % NZ)
     for p in range(PAIRS):
         mixed_t[p] = unstack_heads(acc[p] / total[p])
     mixed = jnp.concatenate([mixed_t[p].T for p in range(PAIRS)], axis=1).astype(BF16)
     aug[...] = (queries[...].astype(F32) + nn(mixed, out_proj[...])).astype(BF16)
-    for cp in ring.values():
-        cp.wait_send()
-    for cp in sent:
-        cp.wait_send()
+    return list(ring.values()) + sent + note_copies
 
 
 def labels_kernel(
-    aug, ints, wcol, labels,
+    aug, onehot, facts, fact, n_send, n_recv, labels,
     d_aug, loss, label_step,
-    rows, served, got, back, back_got, lstage, lgot, dlogit, onehot, lpart, lsend, lrecv,
+    rows, served, got, back, back_got, lstage, lgot, dlogit, lpart, lsend, lrecv,
     psend, prbuf, label_grad, label_got,
     z_send, z_recv, x_send, x_recv, b_send, b_recv, s_send, s_recv, p_send, p_recv, q_send, q_recv,
     g_send, g_recv,
@@ -227,11 +271,6 @@
     y, c, z, x = where_am_i()
     dp = y * 2 + c
     right, left = dev(y, c, (z + 1) % NZ, x), dev(y, c, (z + NZ - 1) % NZ, x)
-    greet(
-        [dev(y, c, z, (x + dx) % NX) for dx in range(1, NX)]
-        + [dev(y, c, (z + d) % NZ, x) for d in range(1, NZ)]
-        + [((dp + d) % 8, z * NX + x) for d in range(1, 8)]
-    )
     ring = {}
 
     def ring_send(way, step, k):
@@ -249,17 +288,11 @@
         for way in (0, 1):
             ring_send(way, 0, k)
     rows[z] = aug[...]
-    query = lax.broadcasted_iota(jnp.int32, (Q, 128), 0)
-
-    def hot(i, carry):
-        onehot[i] = jnp.where(query == ints[i, x, 5:6, :], 1.0, 0.0).astype(BF16)
-        return carry
-
-    lax.fori_loop(0, NZ, hot, 0)
     sent = []
 
-    def serve(zs):
-        picked = tn(onehot[zs], rows[zs]).astype(BF16)
+    def serve(o):
+        zs = (z + o) % NZ
+        picked = tn(onehot[o], rows[zs]).astype(BF16)
         served[zs] = picked.reshape(NX, 2, 16, D)
         got[zs, :, x] = served[zs, x]
         for dx in range(1, NX):
@@ -271,11 +304,12 @@
             cp.start()
             sent.append(cp)
 
-    label = lax.broadcasted_iota(jnp.int32, (64, 512), 1)
+    label = lax.broadcasted_iota(jnp.int32, (64, 512), 1).astype(F32)
     lane = lax.broadcasted_iota(jnp.int32, (NX, 16, 128), 2)
     lstage[...] = jnp.zeros_like(lstage)
 
-    def work(zs):
+    def work(o):
+        zs = (z + o) % NZ
         for dx in range(1, NX):
             remote(
                 served.at[0, 0], got.at[zs, :, 0], x_send.at[dx, zs], x_recv.at[dx, zs], right
@@ -284,11 +318,17 @@
         def cluster(cl, carry):
             entries = got[zs, cl].reshape(64, D)
             logits = nt(entries, labels[cl])
-            want = wcol[zs * 2 + cl]
-            live = (want[:, 4:5] > 0).astype(F32)
-            hit = label == want[:, 0:1]
-            for j in range(1, 4):
-                hit = hit | (label == want[:, j : j + 1])
+            want = facts[:, cl].reshape(64, 128)
+            first = o * 16
+            live = want[:, first + 12 : first + 13]
+            cluster_id = ((z * NX + x) * 2 + cl).astype(F32)
+            hit = None
+            for j in range(4):
+                named = want[:, first + j : first + j + 1]
+                high = want[:, first + 4 + j : first + 5 + j]
+                low = want[:, first + 8 + j : first + 9 + j]
+                one = label == jnp.where(named == cluster_id, high * 256.0 + low, -1.0)
+                hit = one if hit is None else hit | one
             e = jnp.exp(-jnp.abs(logits))
             soft = jnp.maximum(logits, 0.0) + jnp.log1p(e)
             pair_loss = jnp.sum(soft - jnp.where(hit, logits, 0.0), axis=1, keepdims=True) * live
@@ -314,27 +354,29 @@
             cp.start()
             sent.append(cp)
 
-    serve(z)
-    pending = [z]
+    serve(0)
+    for dx in range(1, NX):
+        remote(fact.at[0], facts.at[0], n_send.at[dx], n_recv.at[dx], right).wait_recv()
+    pending = [0]
     for step in range(1, 4):
         for k in range(4):
             for way in (0, 1):
                 ring[way, step - 1, k].wait_recv()
                 if step < 3 or (k < 2) == (way == 0):
                     ring_send(way, step, k)
-        fresh = [(z + NZ - step) % NZ, (z + step) % NZ]
-        for zs in fresh:
-            serve(zs)
-        for zs in pending:
-            work(zs)
+        fresh = [NZ - step, step]
+        for o in fresh:
+            serve(o)
+        for o in pending:
+            work(o)
         pending = fresh
     for k in range(4):
         ring[0 if k < 2 else 1, 3, k].wait_recv()
-    serve((z + 4) % NZ)
-    for zs in pending:
-        work(zs)
-        send_back(zs)
-    work((z + 4) % NZ)
+    serve(4)
+    for o in pending:
+        work(o)
+        send_back((z + o) % NZ)
+    work(4)
     for d in (4, 2, 6, 1, 7, 0):
         send_back((z + d) % NZ)
     loss_copies = []
@@ -345,12 +387,13 @@
         loss_copies.append(cp)
     lgot[x] = lstage[x]
 
-    def partial(zs):
+    def partial(o):
+        zs = (z + o) % NZ
         for dx in range(1, NX):
             remote(
                 back.at[0, :, 0], back_got.at[zs, 0], b_send.at[dx, zs], b_recv.at[dx, zs], right
             ).wait_recv()
-        return nn(onehot[zs], back_got[zs].reshape(128, D))
+        return nn(onehot[o], back_got[zs].reshape(128, D))
 
     label_copies = []
 
@@ -383,13 +426,13 @@
         p_copies[way, step, h] = cp
 
     label_part(0)
-    far = partial((z + 4) % NZ)
+    far = partial(4)
     for way in (0, 1):
         chain_send(way, 0, way, far[way * 64 : way * 64 + 64])
     label_part(1)
     for step in range(1, 4):
         d = 4 - step
-        own = [partial((z + d) % NZ), partial((z + NZ - d) % NZ)]
+        own = [partial(d), partial(NZ - d)]
         for h in (0, 1):
             for way in (h, 1 - h):
                 value = own[way][h * 64 : h * 64 + 64]
@@ -397,7 +440,7 @@
                     p_copies[way, step - 1, h].wait_recv()
                     value = value + prbuf[way, step - 1, h * 64 : h * 64 + 64].astype(F32)
                 chain_send(way, step, h, value)
-    mine = partial(z)
+    mine = partial(0)
     for cp in loss_copies:
         cp.wait()
     losses = jnp.concatenate([lgot[i].reshape(32, 128) for i in range(NX)], axis=0).astype(BF16)
@@ -405,7 +448,7 @@
     lpart[...] = jnp.zeros_like(lpart)
 
     def loss_of(i, carry):
-        lpart[...] = lpart[...] + jnp.where(out_lane == i, nn(onehot[i], losses), 0.0)
+        lpart[...] = lpart[...] + jnp.where(out_lane == (z + i) % NZ, nn(onehot[i], losses), 0.0)
         return carry
 
     lax.fori_loop(0, NZ, loss_of, 0)
@@ -432,12 +475,7 @@
             grad = grad + label_got[cl, i].astype(F32)
         square = jnp.mean(grad * grad, axis=1, keepdims=True)
         label_step[cl] = grad * lax.rsqrt(square + epsilon)
-    for cp in p_copies.values():
-        cp.wait_send()
-    for cp in ring.values():
-        cp.wait_send()
-    for cp in sent:
-        cp.wait_send()
+    return list(p_copies.values()) + list(ring.values()) + sent
 
 
 def grads_kernel(
@@ -449,11 +487,6 @@
     y, c, z, x = where_am_i()
     me = x * 2 + c
     group = [((x + dx) % NX, (c + dc) % 2) for dx, dc in XC]
-    greet(
-        [dev(y, pc, z, px) for px, pc in group[1:]]
-        + [dev((y + d) % NY, c, z, x) for d in range(1, NY)]
-        + [dev(y, c, (z + d) % NZ, x) for d in range(1, NZ)]
-    )
     d_rows = d_aug[...]
     back_proj = nt(d_rows.astype(BF16), out_proj[...]).astype(BF16)
     stack_heads(queries[...], stacked.at[:, 0:256])
@@ -470,7 +503,7 @@
     d_acc[...] = jnp.zeros_like(d_acc)
 
     def compute(zo):
-        w = weight_block(tile_weight[zo])
+        w = weight_block(tile_weight[zo, 0:NX])
 
         def pair(p, carry):
             lanes = pl.ds(pl.multiple_of(p * 128, 128), 128)
@@ -502,7 +535,7 @@
                 gsend.at[zo, 0, 0], ggot.at[0, zo], x_send.at[j, zo], x_recv.at[j, zo],
                 dev(y, c, z, x),
             ).wait_recv()
-        tiles = [asks[s, zo, x] for s in range(8)]
+        tiles = [asks[s, zo * NX + x, 0] for s in range(8)]
 
         def two_tiles(k2, carry):
             sums = []
@@ -594,164 +627,105 @@
 
 
 V = pl.BlockSpec(memory_space=pltpu.VMEM)
-S = pl.BlockSpec(memory_space=pltpu.SMEM)
-
-
-def run(kernel, number, outs, scratch, *args, in_specs=None):
-    return pl.pallas_call(
-        kernel,
-        out_shape=[jax.ShapeDtypeStruct(shape, dtype) for shape, dtype in outs],
-        in_specs=in_specs or [V] * len(args),
-        out_specs=[V] * len(outs),
-        scratch_shapes=scratch,
+
+
+def scratch():
+    names = dict(
+        keys=((32, 64, D), BF16), aug=((Q, D), BF16), mixed_t=((PAIRS, 128, Q), F32),
+        total=((PAIRS, 1, 2 * Q), F32), tile_weight=((NZ, 8, Q), F32), onehot=((NZ, Q, 128), BF16),
+        facts=((NX, 2, 16, 128), F32), ask_smem=None,
+        wanted=((32, 128), jnp.int32), asks=((8, 32, 128), jnp.int32),
+        half=((8, 32, D), BF16), r0=((8, 32, D), BF16), r1=((8, 32, D), BF16),
+        r2=((8, 32, D), BF16), l0=((8, 32, D), BF16), l1=((8, 32, D), BF16),
+        l2=((8, 32, D), BF16), far=((8, 32, D), BF16), stage=((8, NZ, 32, D), BF16),
+        stacked=((PAIRS, 2 * Q, 128), BF16), acc=((PAIRS, 128, 2 * Q), F32),
+        note=((NZ, 24, 128), F32), noted=((NZ, 24, 128), F32), fact=((NX, 2, 16, 128), F32),
+    )
+    first = [
+        pltpu.SMEM((8, 32, 128), jnp.int32) if v is None else pltpu.VMEM(*v)
+        for v in names.values()
+    ]
+    first += [
+        DMA(n)
+        for n in ((2, 4, 4), (2, 4, 4), (8, NZ), (8, NZ), (8,), (8,), (NZ,), (NZ,), (NX,), (NX,))
+    ] + [DMA]
+    second = [
+        pltpu.VMEM((Q, D), F32),
+        pltpu.VMEM((NZ, Q, D), BF16),
+        pltpu.VMEM((NZ, NX, 2, 16, D), BF16),
+        pltpu.VMEM((NZ, 2, NX, 16, D), BF16),
+        pltpu.VMEM((NZ, 2, NX, 16, D), BF16),
+        pltpu.VMEM((NZ, NX, 2, 16, D), BF16),
+        pltpu.VMEM((NX, 2, 16, 128), F32),
+        pltpu.VMEM((NX, 2, 16, 128), F32),
+        pltpu.VMEM((NZ, 2, 64, 512), BF16),
+        pltpu.VMEM((Q, 128), F32),
+        pltpu.VMEM((NZ, 128), F32),
+        pltpu.VMEM((NZ, NZ, 128), F32),
+        pltpu.VMEM((2, 4, Q, D), BF16),
+        pltpu.VMEM((2, 4, Q, D), BF16),
+        pltpu.VMEM((2, 8, 64, D), BF16),
+        pltpu.VMEM((2, 8, 64, D), BF16),
+    ] + [
+        DMA(n)
+        for n in (
+            (2, 4, 4), (2, 4, 4), (NX, NZ), (NX, NZ), (NX, NZ), (NX, NZ), (NX,), (NX,),
+            (2, 4, 2), (2, 4, 2), (NZ,), (NZ,), (2, 8), (2, 8),
+        )
+    ]
+    third = [
+        pltpu.VMEM((PAIRS, 4 * Q, 128), BF16),
+        pltpu.VMEM((PAIRS, 128, 2 * Q), F32),
+        pltpu.VMEM((PAIRS, 1, 2 * Q), F32),
+        pltpu.VMEM((NZ, NX, 2, 32, D), BF16),
+        pltpu.VMEM((8, NZ, 32, D), BF16),
+        pltpu.VMEM((NZ, NY, 4, 16, D), BF16),
+        pltpu.VMEM((NY, NZ, 4, 16, D), BF16),
+        pltpu.VMEM((NZ, 4, 16, D), BF16),
+        pltpu.VMEM((NZ, 4, 16, D), BF16),
+    ] + [DMA(n) for n in ((8, NZ), (8, NZ), (NY, NZ), (NY, NZ), (NZ,), (NZ,))]
+    return first, second, third
+
+
+def whole_kernel(*refs):
+    sizes = [len(part) for part in scratch()]
+    know, numbers, queries, out_proj, labels, loss, query_grad, know_grad, label_step = refs[:9]
+    first = refs[9 : 9 + sizes[0]]
+    second = refs[9 + sizes[0] : 9 + sizes[0] + sizes[1]]
+    third = refs[9 + sizes[0] + sizes[1] :]
+    keys, aug, mixed_t, total, tile_weight, onehot, facts, ask_smem = first[:8]
+    fact, n_send, n_recv = first[23], first[32], first[33]
+    sends = keys_kernel(know, numbers, queries, out_proj, *first)
+    d_aug = second[0]
+    sends += labels_kernel(
+        aug, onehot, facts, fact, n_send, n_recv, labels, d_aug, loss, label_step, *second[1:]
+    )
+    grads_kernel(
+        ask_smem, keys, queries, d_aug, out_proj, mixed_t, total, tile_weight,
+        query_grad, know_grad, *third,
+    )
+    for cp in sends:
+        cp.wait_send()
+
+
+def on_device(queries, tile_ids, knowledge, out_proj, labels, cluster_ids, positive_picks):
+    numbers = jnp.concatenate([tile_ids, cluster_ids, positive_picks], axis=1).T
+    first, second, third = scratch()
+    loss, query_grad, knowledge_grad, label_step = pl.pallas_call(
+        whole_kernel,
+        out_shape=[
+            jax.ShapeDtypeStruct((1, Q), F32),
+            jax.ShapeDtypeStruct((Q, D), F32),
+            jax.ShapeDtypeStruct((8, 8, D), F32),
+            jax.ShapeDtypeStruct((2, 64, D), F32),
+        ],
+        in_specs=[V] * 5,
+        out_specs=[V] * 4,
+        scratch_shapes=first + second + third,
         compiler_params=pltpu.CompilerParams(
-            collective_id=number, has_side_effects=True, vmem_limit_bytes=VMEM_LIMIT
+            collective_id=1, has_side_effects=True, vmem_limit_bytes=VMEM_LIMIT
         ),
-        cost_estimate=pl.CostEstimate(
-            flops=4_000_000_000, bytes_accessed=40_000_000, transcendentals=6_000_000
-        ),
-    )(*args)
-
-
-def prepare(tile_ids, cluster_ids, positive_picks):
-    tiles, ids, picks = tile_ids.T, cluster_ids.T, positive_picks.T
-    owner = jnp.arange(32, dtype=jnp.int32)
-    hits = (tiles // 8)[:, None, :] == owner[None, :, None]
-    tile_weight = jnp.sum(hits.astype(F32), axis=0)
-    wanted = jnp.max(jnp.where(hits, (tiles % 8)[:, None, :], 0), axis=(0, 2))
-    wanted = jnp.pad(wanted.reshape(NZ, NX), ((0, 0), (0, 128 - NX)))
-    cluster = jnp.arange(64, dtype=jnp.int32)
-    member = jnp.any(ids[:, None, :] == cluster[None, :, None], axis=0)
-    before = (jnp.arange(Q)[:, None] < jnp.arange(Q)[None, :]).astype(BF16)
-    rank = jnp.dot(member.astype(BF16), before, preferred_element_type=F32).astype(jnp.int32)
-    rank = jnp.where(member, rank, -1)
-    slot = jnp.arange(16, dtype=jnp.int32)
-    held = rank[:, None, :] == slot[None, :, None]
-    query = jnp.arange(Q, dtype=jnp.int32)
-    slot_query = Q + jnp.sum(jnp.where(held, query - Q, 0), axis=2)
-    live = (slot_query < Q).astype(jnp.int32)
-    column = picks // 512
-    pick_cluster = jnp.sum(
-        jnp.where(column[:, None, :] == jnp.arange(4)[None, :, None], ids[None], 0), axis=1
-    )
-    pick_label = picks % 512 + 1
-    wanted_label = [
-        jnp.sum(
-            jnp.where(
-                held & (pick_cluster[j][None, None, :] == cluster[:, None, None]),
-                pick_label[j],
-                0,
-            ),
-            axis=2,
-        )
-        - 1
-        for j in range(4)
-    ]
-    parts = [a.reshape(NZ, NX, 1, 32) for a in wanted_label + [live]]
-    parts = jnp.pad(jnp.concatenate(parts, axis=2), ((0, 0), (0, 0), (0, 0), (0, 96)))
-    slots = jnp.broadcast_to(slot_query.reshape(NZ, 1, 1, 128), (NZ, NX, 1, 128))
-    msg = jnp.concatenate([parts, slots, jnp.zeros((NZ, NX, 2, 128), jnp.int32)], axis=2)
-    return tile_weight.reshape(NZ, NX, Q), wanted, msg.transpose(1, 0, 2, 3)
-
-
-def on_device(queries, tile_ids, knowledge, out_proj, labels, cluster_ids, positive_picks):
-    tile_weight, wanted, msg = prepare(tile_ids, cluster_ids, positive_picks)
-    keys, aug, mixed_t, total, asks, ints = run(
-        keys_kernel,
-        1,
-        [
-            ((32, 64, D), BF16),
-            ((Q, D), BF16),
-            ((PAIRS, 128, Q), F32),
-            ((PAIRS, 1, 2 * Q), F32),
-            ((8, 8, 128), jnp.int32),
-            ((NZ, NX, 8, 128), jnp.int32),
-        ],
-        [
-            *[pltpu.VMEM((8, 32, D), BF16) for _ in range(8)],
-            pltpu.VMEM((8, NZ, 32, D), BF16),
-            pltpu.VMEM((PAIRS, 2 * Q, 128), BF16),
-            pltpu.VMEM((PAIRS, 128, 2 * Q), F32),
-            pltpu.VMEM((NX, NZ, 8, 128), jnp.int32),
-            pltpu.SMEM((8, 8, 128), jnp.int32),
-            DMA((2, 4, 4)),
-            DMA((2, 4, 4)),
-            DMA((8, NZ)),
-            DMA((8, NZ)),
-            DMA((8,)),
-            DMA((8,)),
-            DMA((NX,)),
-            DMA((NX,)),
-            DMA((NZ,)),
-            DMA((NZ,)),
-            DMA,
-        ],
-        knowledge, wanted, queries, tile_weight, out_proj, msg,
-    )
-    wcol = ints[:, :, :5, :32].reshape(NZ, NX, 5, 2, 16).transpose(0, 3, 1, 4, 2)
-    wcol = jnp.pad(wcol.reshape(16, 64, 5), ((0, 0), (0, 0), (0, 3)))
-    d_aug, loss, label_step = run(
-        labels_kernel,
-        2,
-        [((Q, D), F32), ((1, Q), F32), ((2, 64, D), F32)],
-        [
-            pltpu.VMEM((NZ, Q, D), BF16),
-            pltpu.VMEM((NZ, NX, 2, 16, D), BF16),
-            pltpu.VMEM((NZ, 2, NX, 16, D), BF16),
-            pltpu.VMEM((NZ, 2, NX, 16, D), BF16),
-            pltpu.VMEM((NZ, NX, 2, 16, D), BF16),
-            pltpu.VMEM((NX, 2, 16, 128), F32),
-            pltpu.VMEM((NX, 2, 16, 128), F32),
-            pltpu.VMEM((NZ, 2, 64, 512), BF16),
-            pltpu.VMEM((NZ, Q, 128), BF16),
-            pltpu.VMEM((Q, 128), F32),
-            pltpu.VMEM((NZ, 128), F32),
-            pltpu.VMEM((NZ, NZ, 128), F32),
-            pltpu.VMEM((2, 4, Q, D), BF16),
-            pltpu.VMEM((2, 4, Q, D), BF16),
-            pltpu.VMEM((2, 8, 64, D), BF16),
-            pltpu.VMEM((2, 8, 64, D), BF16),
-            DMA((2, 4, 4)),
-            DMA((2, 4, 4)),
-            DMA((NX, NZ)),
-            DMA((NX, NZ)),
-            DMA((NX, NZ)),
-            DMA((NX, NZ)),
-            DMA((NX,)),
-            DMA((NX,)),
-            DMA((2, 4, 2)),
-            DMA((2, 4, 2)),
-            DMA((NZ,)),
-            DMA((NZ,)),
-            DMA((2, 8)),
-            DMA((2, 8)),
-        ],
-        aug, ints, wcol, labels,
-    )
-    query_grad, knowledge_grad = run(
-        grads_kernel,
-        3,
-        [((Q, D), F32), ((8, 8, D), F32)],
-        [
-            pltpu.VMEM((PAIRS, 4 * Q, 128), BF16),
-            pltpu.VMEM((PAIRS, 128, 2 * Q), F32),
-            pltpu.VMEM((PAIRS, 1, 2 * Q), F32),
-            pltpu.VMEM((NZ, NX, 2, 32, D), BF16),
-            pltpu.VMEM((8, NZ, 32, D), BF16),
-            pltpu.VMEM((NZ, NY, 4, 16, D), BF16),
-            pltpu.VMEM((NY, NZ, 4, 16, D), BF16),
-            pltpu.VMEM((NZ, 4, 16, D), BF16),
-            pltpu.VMEM((NZ, 4, 16, D), BF16),
-            DMA((8, NZ)),
-            DMA((8, NZ)),
-            DMA((NY, NZ)),
-            DMA((NY, NZ)),
-            DMA((NZ,)),
-            DMA((NZ,)),
-        ],
-        asks, keys, queries, d_aug, out_proj, mixed_t, total, tile_weight,
-        in_specs=[S] + [V] * 7,
-    )
+    )(knowledge, numbers, queries, out_proj, labels)
     return (loss[0], query_grad, knowledge_grad, label_step)
 
 

time: 202 us -> 181 us (0.90)
  other arithmetic: 8.64 us -> 1.32 us
  Pallas kernels: 178 us -> 171 us
  local copies, waits for them, and re-layouts: 11.9 us -> 6.24 us
    pallas_call x3 -> x1, Pallas kernels: 178 us -> 171 us  [on_device(): pl.pallas_call(whole_kernel, out_shape=[jax.ShapeDtypeStruct((1, Q), F32)...]
    reduce_sum x3 -> x0, other arithmetic: 6.19 us -> none  [the longest x1 5.47 us: prepare(): slot_query = Q + jnp.sum(jnp.where(held, query - Q, 0), axis=2)]
    transpose x1 -> x0, local copies, waits for them, and re-layouts: 2.15 us -> none  [on_device(): ints[:, :, :5, :32].reshape(NZ, NX, 5, 2, 16).transpose(0, 3, 1, 4, 2)]
    unnamed x16 -> x4, local copies, waits for them, and re-layouts: 5.41 us -> 6.24 us
where the time goes in v3:
time: 181 us; the launch traced here: 179 us
  Pallas kernels  171 us (94%)
  local copies, waits for them, and re-layouts  6.24 us (3%)
    pallas_call x1, Pallas kernels, on_device(): pl.pallas_call(whole_kernel, out_shape=[jax.ShapeDtypeStruct((1, Q), F32)...  171 us
    unnamed x4, local copies, waits for them, and re-layouts  6.24 us

profile of v3, /device:TPU:16, one launch (start us, length us, event | category | flops | bytes accessed | tf_op | source)
XLA Modules:
  0.0 179.4 jit_solution(297197536271121545)
XLA Ops:
  0.6 1.3 add_bitcast_fusion.refs_1_
  2.0 171.2 %shard_map.102 = (f32[1,128]{1,0:T(1,128)}, f32[128,768]{1,0:T(8,128)}, f32[8,8,768]{2,1,0:T(8,128)}, f32[2,64,768]{2,1,0:T(8,128)}) custom-call(bf16[8,64,768]{2,1,0:T(8,128)(2,1)} %refs_0_.1, s32[12,128]{1,0:T(8,128)} %add_bitcast_fusion.refs_1_, bf16[128,768]{1,0:T(8,128)(2,1)} %refs_2_.1, bf16[768,768]{1,0:T(8,128)(2,1)} %refs_3_.1, ...), custom_call_target="tpu_custom_call" | custom-call | tf_op jit(solution)/shard_map/pallas_call | solution.py:714
  173.1 1.1 copy.15
  174.2 1.8 copy.16
  176.0 1.6 copy.17
  177.6 1.8 copy.18

commit v4 on v3

--- a/solution.py
+++ b/solution.py
@@ -33,7 +33,7 @@
     barrier = pltpu.get_barrier_semaphore()
     for peer in peers:
         pl.semaphore_signal(barrier, inc=1, device_id=peer, device_id_type=MESH)
-    pl.semaphore_wait(barrier, len(peers))
+    return lambda: pl.semaphore_wait(barrier, len(peers))
 
 
 def remote(src, dst, send, recv, to):
@@ -77,35 +77,26 @@
 def keys_kernel(
     know, numbers, queries, out_proj,
     keys, aug, mixed_t, total, tile_weight, onehot, facts, ask_smem,
-    wanted, asks, half, r0, r1, r2, l0, l1, l2, far, stage, stacked, acc, note, noted, fact,
+    wanted, asks, ask_row,
+    half0, half1, r00, r01, r10, r11, r20, r21, l00, l01, l10, l11, l20, l21, far0, far1,
+    stage, stacked, acc, note, noted, fact,
     z_send, z_recv, x_send, x_recv, a_send, a_recv, m_send, m_recv, n_send, n_recv, l_sem,
 ):
     y, c, z, x = where_am_i()
     dp = y * 2 + c
     me = x * 2 + c
+    start, far = (half0, half1), (far0, far1)
+    r0, r1, r2 = (r00, r01), (r10, r11), (r20, r21)
+    l0, l1, l2 = (l00, l01), (l10, l11), (l20, l21)
     right, left = dev(y, c, (z + 1) % NZ, x), dev(y, c, (z + NZ - 1) % NZ, x)
     group = [((x + dx) % NX, (c + dc) % 2) for dx, dc in XC]
-    greet(
+    everyone_in = greet(
         [dev(y, pc, z, px) for px, pc in group[1:]]
         + [dev(y, c, (z + d) % NZ, x) for d in range(1, NZ)]
         + [((dp + d) % 8, z * NX + x) for d in range(1, 8)]
     )
-    half[...] = know[:, pl.ds(pl.multiple_of(c * 32, 32), 32), :]
-    ring = {}
-    slots = ((half, r0, r1, r2, far), (half, l0, l1, l2, far))
-
-    def ring_send(way, step, k):
-        piece = pl.ds(k * 2, 2)
-        cp = remote(
-            slots[way][step].at[piece], slots[way][step + 1].at[piece],
-            z_send.at[way, step, k], z_recv.at[way, step, k], right if way == 0 else left,
-        )
-        cp.start()
-        ring[way, step, k] = cp
-
-    for k in range(4):
-        for way in (0, 1):
-            ring_send(way, 0, k)
+    for h in (0, 1):
+        start[h][...] = know[:, pl.ds(pl.multiple_of(c * 32 + h * 16, 16), 16), :]
     owner = lax.broadcasted_iota(jnp.int32, (32, Q), 0)
     weight, tile = jnp.zeros((32, Q), F32), jnp.zeros((32, Q), jnp.int32)
     for r in range(4):
@@ -113,14 +104,11 @@
         hit = (named >> 3) == owner
         weight = weight + jnp.where(hit, 1.0, 0.0)
         tile = jnp.maximum(tile, jnp.where(hit, named & 7, 0))
-    wanted[...] = jnp.broadcast_to(jnp.max(tile, axis=1, keepdims=True), (32, 128))
+    tile = jnp.broadcast_to(jnp.max(tile, axis=1, keepdims=True), (32, 128)).reshape(NZ, NX, 128)
+    for i in range(NX):
+        wanted[i] = tile[:, i]
     ask_copies = []
-    for j in range(1, 8):
-        px, pc = group[j]
-        cp = remote(wanted, asks.at[me], a_send.at[j], a_recv.at[j], dev(y, pc, z, px))
-        cp.start()
-        ask_copies.append(cp)
-    asks[me] = wanted[...]
+    asks[me] = wanted[x]
     for zo in range(NZ):
         tile_weight[zo, 0:NX] = weight[zo * NX : zo * NX + NX]
     cluster = lax.broadcasted_iota(jnp.int32, (64, Q), 0)
@@ -147,6 +135,30 @@
     for i in range(NZ):
         note[i, 0:8] = rank[i * 8 : i * 8 + 8]
         note[i, 8:24] = columns
+    stack_heads(queries[...], stacked)
+    acc[...] = jnp.zeros_like(acc)
+    total[...] = jnp.zeros_like(total)
+    everyone_in()
+    for j in range(1, 8):
+        px, pc = group[j]
+        cp = remote(wanted.at[px], asks.at[me], a_send.at[j], a_recv.at[j], dev(y, pc, z, px))
+        cp.start()
+        ask_copies.append(cp)
+    ring = {}
+    slots = ((start, r0, r1, r2, far), (start, l0, l1, l2, far))
+
+    def ring_send(way, step, k):
+        h, piece = k // 2, pl.ds((k % 2) * 4, 4)
+        cp = remote(
+            slots[way][step][h].at[piece], slots[way][step + 1][h].at[piece],
+            z_send.at[way, step, k], z_recv.at[way, step, k], right if way == 0 else left,
+        )
+        cp.start()
+        ring[way, step, k] = cp
+
+    for k in range(4):
+        for way in (0, 1):
+            ring_send(way, 0, k)
     note_copies = []
     for d in range(1, NZ):
         zp = (z + d) % NZ
@@ -180,37 +192,34 @@
             cp.start()
             note_copies.append(cp)
 
-    stack_heads(queries[...], stacked)
-    acc[...] = jnp.zeros_like(acc)
-    total[...] = jnp.zeros_like(total)
     for cp in ask_copies:
         cp.wait()
-    cp = pltpu.make_async_copy(asks, ask_smem, l_sem)
+    peer = lax.broadcasted_iota(jnp.int32, (NZ, 128), 1)
+    table = jnp.zeros((NZ, 128), jnp.int32)
+    for i in range(8):
+        table = jnp.where(peer == i, asks[i], table)
+    ask_row[...] = table
+    cp = pltpu.make_async_copy(ask_row, ask_smem, l_sem)
     cp.start()
     cp.wait()
-    sent = []
-
-    def serve(zo, shard):
-        row = pl.ds(pl.multiple_of(c * 32, 32), 32)
+
+    def serve(zo, h, shard):
+        row = pl.ds(pl.multiple_of(c * 32 + h * 16, 16), 16)
         for j, (px, pc) in enumerate(group):
-            tile = jnp.clip(ask_smem[px * 2 + pc, zo * NX + x, 0], 0, 7)
+            tile = jnp.clip(ask_smem[zo, px * 2 + pc], 0, 7)
             if j == 0:
                 keys[zo * NX + x, row] = shard[tile]
                 continue
-            stage[j, zo] = shard[tile]
+            stage[j, zo, h] = shard[tile]
             cp = remote(
-                stage.at[j, zo], keys.at[zo * NX + x, row], x_send.at[j, zo], x_recv.at[j, zo],
-                dev(y, pc, z, px),
+                stage.at[j, zo, h], keys.at[zo * NX + x, row], x_send.at[0],
+                x_recv.at[zo], dev(y, pc, z, px),
             )
             cp.start()
-            sent.append(cp)
 
     def arrived(zo):
-        for j in range(1, 8):
-            row = pl.ds(0, 32)
-            remote(
-                stage.at[j, zo], keys.at[zo * NX, row], x_send.at[j, zo], x_recv.at[j, zo], right
-            ).wait_recv()
+        pieces = stage.at[pl.ds(0, 7), zo]
+        remote(pieces, pieces, x_send.at[0], x_recv.at[zo], right).wait_recv()
 
     def attend(zo):
         w = weight_block(tile_weight[zo, 0:NX])
@@ -229,25 +238,29 @@
     def wait_step(way, step, k):
         ring[way, step, k].wait_recv()
 
-    serve(z, half)
+    for h in (0, 1):
+        serve(z, h, start[h])
     pending = [z]
     for step in range(1, 4):
-        for k in range(4):
+        fresh = [(z + NZ - step) % NZ, (z + step) % NZ]
+        for h in (0, 1):
+            for k in (2 * h, 2 * h + 1):
+                for way in (0, 1):
+                    wait_step(way, step - 1, k)
+                    if step < 3 or (k < 2) == (way == 0):
+                        ring_send(way, step, k)
             for way in (0, 1):
-                wait_step(way, step - 1, k)
-                if step < 3 or (k < 2) == (way == 0):
-                    ring_send(way, step, k)
-        serve((z + NZ - step) % NZ, slots[0][step])
-        serve((z + step) % NZ, slots[1][step])
+                serve(fresh[way], h, slots[way][step][h])
         for zo in pending:
             arrived(zo)
             attend(zo)
         if step == 1:
             slots_and_facts()
-        pending = [(z + NZ - step) % NZ, (z + step) % NZ]
-    for k in range(4):
-        wait_step(0 if k < 2 else 1, 3, k)
-    serve((z + 4) % NZ, far)
+        pending = fresh
+    for h in (0, 1):
+        for k in (2 * h, 2 * h + 1):
+            wait_step(h, 3, k)
+        serve((z + 4) % NZ, h, far[h])
     for zo in pending:
         arrived(zo)
         attend(zo)
@@ -257,7 +270,8 @@
         mixed_t[p] = unstack_heads(acc[p] / total[p])
     mixed = jnp.concatenate([mixed_t[p].T for p in range(PAIRS)], axis=1).astype(BF16)
     aug[...] = (queries[...].astype(F32) + nn(mixed, out_proj[...])).astype(BF16)
-    return list(ring.values()) + sent + note_copies
+    pieces = stage.at[pl.ds(0, 7)]
+    return list(ring.values()) + [remote(pieces, pieces, x_send.at[0], x_recv.at[0], right)] + note_copies
 
 
 def labels_kernel(
@@ -521,28 +535,25 @@
             return carry
 
         lax.fori_loop(0, PAIRS, pair, 0)
-        ggot[me, zo] = gsend[zo, x, c]
+        ggot[zo, me] = gsend[zo, x, c]
         for j in range(1, 8):
             px, pc = group[j]
             remote(
-                gsend.at[zo, px, pc], ggot.at[me, zo], x_send.at[j, zo], x_recv.at[j, zo],
+                gsend.at[zo, px, pc], ggot.at[zo, me], x_send.at[0], x_recv.at[zo],
                 dev(y, pc, z, px),
             ).start()
 
     def gather_tiles(zo):
-        for j in range(1, 8):
-            remote(
-                gsend.at[zo, 0, 0], ggot.at[0, zo], x_send.at[j, zo], x_recv.at[j, zo],
-                dev(y, c, z, x),
-            ).wait_recv()
-        tiles = [asks[s, zo * NX + x, 0] for s in range(8)]
+        pieces = ggot.at[zo, pl.ds(0, 7)]
+        remote(pieces, pieces, x_send.at[0], x_recv.at[zo], dev(y, c, z, x)).wait_recv()
+        tiles = [asks[zo, s] for s in range(8)]
 
         def two_tiles(k2, carry):
             sums = []
             for k in range(2):
                 value = jnp.zeros((32, D), F32)
                 for s in range(8):
-                    value = value + ggot[s, zo].astype(F32) * jnp.where(
+                    value = value + ggot[zo, s].astype(F32) * jnp.where(
                         tiles[s] == k2 * 2 + k, 1.0, 0.0
                     )
                 sums.append(value.reshape(NY, 1, 8, D))
@@ -551,23 +562,20 @@
             return carry
 
         lax.fori_loop(0, 4, two_tiles, 0)
-        ygot[y, zo] = ysend[zo, y]
+        ygot[zo, y] = ysend[zo, y]
         for d in range(1, NY):
             py = (y + d) % NY
             remote(
-                ysend.at[zo, py], ygot.at[y, zo], y_send.at[d, zo], y_recv.at[d, zo],
+                ysend.at[zo, py], ygot.at[zo, y], y_send.at[0], y_recv.at[zo],
                 dev(py, c, z, x),
             ).start()
 
     def gather_shards(zo, own):
-        for d in range(1, NY):
-            remote(
-                ysend.at[zo, 0], ygot.at[0, zo], y_send.at[d, zo], y_recv.at[d, zo],
-                dev(y, c, z, x),
-            ).wait_recv()
-        value = ygot[0, zo].astype(F32)
+        pieces = ygot.at[zo, pl.ds(0, 3)]
+        remote(pieces, pieces, y_send.at[0], y_recv.at[zo], dev(y, c, z, x)).wait_recv()
+        value = ygot[zo, 0].astype(F32)
         for i in range(1, NY):
-            value = value + ygot[i, zo].astype(F32)
+            value = value + ygot[zo, i].astype(F32)
         zsend[zo] = value.astype(BF16)
 
         @pl.when(own == 0)
@@ -608,20 +616,10 @@
         value = value + zgot[i].astype(F32)
     know_grad[...] = value.reshape(8, 8, D)
 
-    def drain(zo, carry):
-        for j in range(1, 8):
-            remote(
-                gsend.at[zo, 0, 0], ggot.at[0, zo], x_send.at[j, zo], x_recv.at[j, zo],
-                dev(y, c, z, x),
-            ).wait_send()
-        for d in range(1, NY):
-            remote(
-                ysend.at[zo, 0], ygot.at[0, zo], y_send.at[d, zo], y_recv.at[d, zo],
-                dev(y, c, z, x),
-            ).wait_send()
-        return carry
-
-    lax.fori_loop(0, NZ, drain, 0)
+    pieces = ggot.at[pl.ds(0, 7)]
+    remote(pieces, pieces, x_send.at[0], x_recv.at[0], dev(y, c, z, x)).wait_send()
+    pieces = ygot.at[pl.ds(0, 6)]
+    remote(pieces, pieces, y_send.at[0], y_recv.at[0], dev(y, c, z, x)).wait_send()
     for d in range(1, NZ):
         remote(zsend.at[0], zgot.at[0], z_send.at[d], z_recv.at[d], dev(y, c, z, x)).wait_send()
 
@@ -634,20 +632,20 @@
         keys=((32, 64, D), BF16), aug=((Q, D), BF16), mixed_t=((PAIRS, 128, Q), F32),
         total=((PAIRS, 1, 2 * Q), F32), tile_weight=((NZ, 8, Q), F32), onehot=((NZ, Q, 128), BF16),
         facts=((NX, 2, 16, 128), F32), ask_smem=None,
-        wanted=((32, 128), jnp.int32), asks=((8, 32, 128), jnp.int32),
-        half=((8, 32, D), BF16), r0=((8, 32, D), BF16), r1=((8, 32, D), BF16),
-        r2=((8, 32, D), BF16), l0=((8, 32, D), BF16), l1=((8, 32, D), BF16),
-        l2=((8, 32, D), BF16), far=((8, 32, D), BF16), stage=((8, NZ, 32, D), BF16),
+        wanted=((NX, NZ, 128), jnp.int32), asks=((8, NZ, 128), jnp.int32),
+        ask_row=((NZ, 128), jnp.int32),
+        **{"b%d" % i: ((8, 16, D), BF16) for i in range(16)},
+        stage=((8, NZ, 2, 16, D), BF16),
         stacked=((PAIRS, 2 * Q, 128), BF16), acc=((PAIRS, 128, 2 * Q), F32),
         note=((NZ, 24, 128), F32), noted=((NZ, 24, 128), F32), fact=((NX, 2, 16, 128), F32),
     )
     first = [
-        pltpu.SMEM((8, 32, 128), jnp.int32) if v is None else pltpu.VMEM(*v)
+        pltpu.SMEM((NZ, 128), jnp.int32) if v is None else pltpu.VMEM(*v)
         for v in names.values()
     ]
     first += [
         DMA(n)
-        for n in ((2, 4, 4), (2, 4, 4), (8, NZ), (8, NZ), (8,), (8,), (NZ,), (NZ,), (NX,), (NX,))
+        for n in ((2, 4, 4), (2, 4, 4), (1,), (NZ,), (8,), (8,), (NZ,), (NZ,), (NX,), (NX,))
     ] + [DMA]
     second = [
         pltpu.VMEM((Q, D), F32),
@@ -678,12 +676,12 @@
         pltpu.VMEM((PAIRS, 128, 2 * Q), F32),
         pltpu.VMEM((PAIRS, 1, 2 * Q), F32),
         pltpu.VMEM((NZ, NX, 2, 32, D), BF16),
-        pltpu.VMEM((8, NZ, 32, D), BF16),
+        pltpu.VMEM((NZ, 8, 32, D), BF16),
         pltpu.VMEM((NZ, NY, 4, 16, D), BF16),
-        pltpu.VMEM((NY, NZ, 4, 16, D), BF16),
+        pltpu.VMEM((NZ, NY, 4, 16, D), BF16),
         pltpu.VMEM((NZ, 4, 16, D), BF16),
         pltpu.VMEM((NZ, 4, 16, D), BF16),
-    ] + [DMA(n) for n in ((8, NZ), (8, NZ), (NY, NZ), (NY, NZ), (NZ,), (NZ,))]
+    ] + [DMA(n) for n in ((1,), (NZ,), (1,), (NZ,), (NZ,), (NZ,))]
     return first, second, third
 
 
@@ -694,7 +692,7 @@
     second = refs[9 + sizes[0] : 9 + sizes[0] + sizes[1]]
     third = refs[9 + sizes[0] + sizes[1] :]
     keys, aug, mixed_t, total, tile_weight, onehot, facts, ask_smem = first[:8]
-    fact, n_send, n_recv = first[23], first[32], first[33]
+    fact, n_send, n_recv = first[32], first[41], first[42]
     sends = keys_kernel(know, numbers, queries, out_proj, *first)
     d_aug = second[0]
     sends += labels_kernel(
@@ -708,17 +706,27 @@
         cp.wait_send()
 
 
+def hand_out(*refs):
+    ins, outs, sems = refs[:4], refs[4:8], refs[8]
+    copies = [pltpu.make_async_copy(ins[i], outs[i], sems.at[i]) for i in range(4)]
+    for cp in copies:
+        cp.start()
+    for cp in copies:
+        cp.wait()
+
+
 def on_device(queries, tile_ids, knowledge, out_proj, labels, cluster_ids, positive_picks):
     numbers = jnp.concatenate([tile_ids, cluster_ids, positive_picks], axis=1).T
     first, second, third = scratch()
-    loss, query_grad, knowledge_grad, label_step = pl.pallas_call(
+    shapes = [
+        jax.ShapeDtypeStruct((1, Q), F32),
+        jax.ShapeDtypeStruct((Q, D), F32),
+        jax.ShapeDtypeStruct((8, 8, D), F32),
+        jax.ShapeDtypeStruct((2, 64, D), F32),
+    ]
+    results = pl.pallas_call(
         whole_kernel,
-        out_shape=[
-            jax.ShapeDtypeStruct((1, Q), F32),
-            jax.ShapeDtypeStruct((Q, D), F32),
-            jax.ShapeDtypeStruct((8, 8, D), F32),
-            jax.ShapeDtypeStruct((2, 64, D), F32),
-        ],
+        out_shape=shapes,
         in_specs=[V] * 5,
         out_specs=[V] * 4,
         scratch_shapes=first + second + third,
@@ -726,6 +734,13 @@
             collective_id=1, has_side_effects=True, vmem_limit_bytes=VMEM_LIMIT
         ),
     )(knowledge, numbers, queries, out_proj, labels)
+    loss, query_grad, knowledge_grad, label_step = pl.pallas_call(
+        hand_out,
+        out_shape=shapes,
+        in_specs=[V] * 4,
+        out_specs=[pl.BlockSpec(memory_space=pl.ANY)] * 4,
+        scratch_shapes=[DMA((4,))],
+    )(*results)
     return (loss[0], query_grad, knowledge_grad, label_step)
 
 

time: 181 us -> 171 us (0.945)
  local copies, waits for them, and re-layouts: 6.24 us -> 0 us
  Pallas kernels: 171 us -> 166 us
    unnamed x4 -> x0, local copies, waits for them, and re-layouts: 6.24 us -> none
    pallas_call x1 -> x2, Pallas kernels: 171 us -> 166 us  [the longest x1 164 us: on_device(): pl.pallas_call(whole_kernel, out_shape=shapes, in_specs=[V] * 5, out_spec...]
where the time goes in v4:
time: 171 us; the launch traced here: 168 us
  Pallas kernels  166 us (97%)
    pallas_call x1, Pallas kernels, on_device(): pl.pallas_call(whole_kernel, out_shape=shapes, in_specs=[V] * 5, out_spec...  164 us

profile of v4, /device:TPU:16, one launch (start us, length us, event | category | flops | bytes accessed | tf_op | source)
XLA Modules:
  0.0 168.3 jit_solution(6993684215409660885)
XLA Ops:
  0.6 1.3 add_bitcast_fusion.refs_1_
  2.0 164.1 %shard_map.102 = (f32[1,128]{1,0:T(1,128)}, f32[128,768]{1,0:T(8,128)}, f32[8,8,768]{2,1,0:T(8,128)}, f32[2,64,768]{2,1,0:T(8,128)}) custom-call(bf16[8,64,768]{2,1,0:T(8,128)(2,1)} %refs_0_.1, s32[12,128]{1,0:T(8,128)} %add_bitcast_fusion.refs_1_, bf16[128,768]{1,0:T(8,128)(2,1)} %refs_2_.1, bf16[768,768]{1,0:T(8,128)(2,1)} %refs_3_.1, ...), custom_call_target="tpu_custom_call" | custom-call | tf_op jit(solution)/shard_map/pallas_call | solution.py:727
  166.1 2.2 %shard_map.103 = (f32[1,128]{1,0:T(1,128)}, f32[128,768]{1,0:T(8,128)}, f32[8,8,768]{2,1,0:T(8,128)}, f32[2,64,768]{2,1,0:T(8,128)}) custom-call(f32[1,128]{1,0:T(1,128)} %get-tuple-element.12.refs_0_, f32[128,768]{1,0:T(8,128)} %get-tuple-element.13.refs_1_, f32[8,8,768]{2,1,0:T(8,128)} %get-tuple-element.14.refs_2_, f32[2,64,768]{2,1,0:T(8,128)} %get-tuple-element.15.refs_3_), custom_call_target="tpu_custom_call" | custom-call | tf_op jit(solution)/shard_map/pallas_call | solution.py:737

commit v5 on v4

--- a/solution.py
+++ b/solution.py
@@ -111,6 +111,27 @@
     asks[me] = wanted[x]
     for zo in range(NZ):
         tile_weight[zo, 0:NX] = weight[zo * NX : zo * NX + NX]
+    everyone_in()
+    for j in range(1, 8):
+        px, pc = group[j]
+        cp = remote(wanted.at[px], asks.at[me], a_send.at[j], a_recv.at[j], dev(y, pc, z, px))
+        cp.start()
+        ask_copies.append(cp)
+    ring = {}
+    slots = ((start, r0, r1, r2, far), (start, l0, l1, l2, far))
+
+    def ring_send(way, step, k):
+        h, piece = k // 2, pl.ds((k % 2) * 4, 4)
+        cp = remote(
+            slots[way][step][h].at[piece], slots[way][step + 1][h].at[piece],
+            z_send.at[way, step, k], z_recv.at[way, step, k], right if way == 0 else left,
+        )
+        cp.start()
+        ring[way, step, k] = cp
+
+    for k in range(4):
+        for way in (0, 1):
+            ring_send(way, 0, k)
     cluster = lax.broadcasted_iota(jnp.int32, (64, Q), 0)
     ids = [numbers[4 + i : 5 + i, :] for i in range(4)]
     member = ids[0] == cluster
@@ -138,27 +159,6 @@
     stack_heads(queries[...], stacked)
     acc[...] = jnp.zeros_like(acc)
     total[...] = jnp.zeros_like(total)
-    everyone_in()
-    for j in range(1, 8):
-        px, pc = group[j]
-        cp = remote(wanted.at[px], asks.at[me], a_send.at[j], a_recv.at[j], dev(y, pc, z, px))
-        cp.start()
-        ask_copies.append(cp)
-    ring = {}
-    slots = ((start, r0, r1, r2, far), (start, l0, l1, l2, far))
-
-    def ring_send(way, step, k):
-        h, piece = k // 2, pl.ds((k % 2) * 4, 4)
-        cp = remote(
-            slots[way][step][h].at[piece], slots[way][step + 1][h].at[piece],
-            z_send.at[way, step, k], z_recv.at[way, step, k], right if way == 0 else left,
-        )
-        cp.start()
-        ring[way, step, k] = cp
-
-    for k in range(4):
-        for way in (0, 1):
-            ring_send(way, 0, k)
     note_copies = []
     for d in range(1, NZ):
         zp = (z + d) % NZ
@@ -233,7 +233,7 @@
             acc[p] = acc[p] + tn(k, raw.astype(BF16))
             return carry
 
-        lax.fori_loop(0, PAIRS, pair, 0)
+        lax.fori_loop(0, PAIRS, pair, 0, unroll=2)
 
     def wait_step(way, step, k):
         ring[way, step, k].wait_recv()
@@ -534,7 +534,7 @@
                 gsend[zo, :, side, :, lanes] = grad[:, :, side].reshape(NX, 32, 128).astype(BF16)
             return carry
 
-        lax.fori_loop(0, PAIRS, pair, 0)
+        lax.fori_loop(0, PAIRS, pair, 0, unroll=2)
         ggot[zo, me] = gsend[zo, x, c]
         for j in range(1, 8):
             px, pc = group[j]
@@ -596,17 +596,17 @@
         def _():
             compute((z + offset(i)) % NZ)
 
-        @pl.when((i >= 3) & (i < 11))
+        @pl.when((i >= 2) & (i < 10))
         def _():
-            gather_tiles((z + offset(i - 3)) % NZ)
-
-        @pl.when(i >= 5)
+            gather_tiles((z + offset(i - 2)) % NZ)
+
+        @pl.when((i >= 4) & (i < 12))
         def _():
-            gather_shards((z + offset(i - 5)) % NZ, offset(i - 5))
+            gather_shards((z + offset(i - 4)) % NZ, offset(i - 4))
 
         return carry
 
-    lax.fori_loop(0, 13, body, 0)
+    lax.fori_loop(0, 12, body, 0)
     d_query = jnp.concatenate([unstack_heads(d_acc[p]).T for p in range(PAIRS)], axis=1)
     query_grad[...] = d_rows + d_query
     for d in range(1, NZ):

time: 171 us -> 169 us (0.988)
  Pallas kernels: 166 us -> 164 us
    pallas_call x1, Pallas kernels: 164 us -> 162 us  [on_device(): pl.pallas_call(whole_kernel, out_shape=shapes, in_specs=[V] * 5, out_spec...]
where the time goes in v5:
time: 169 us; the launch traced here: 166 us
  Pallas kernels  164 us (97%)
    pallas_call x1, Pallas kernels, on_device(): pl.pallas_call(whole_kernel, out_shape=shapes, in_specs=[V] * 5, out_spec...  162 us

profile of v5, /device:TPU:16, one launch (start us, length us, event | category | flops | bytes accessed | tf_op | source)
XLA Modules:
  0.0 166.3 jit_solution(18088100224167307787)
XLA Ops:
  0.6 1.3 add_bitcast_fusion.refs_1_
  2.0 162.2 %shard_map.102 = (f32[1,128]{1,0:T(1,128)}, f32[128,768]{1,0:T(8,128)}, f32[8,8,768]{2,1,0:T(8,128)}, f32[2,64,768]{2,1,0:T(8,128)}) custom-call(bf16[8,64,768]{2,1,0:T(8,128)(2,1)} %refs_0_.1, s32[12,128]{1,0:T(8,128)} %add_bitcast_fusion.refs_1_, bf16[128,768]{1,0:T(8,128)(2,1)} %refs_2_.1, bf16[768,768]{1,0:T(8,128)(2,1)} %refs_3_.1, ...), custom_call_target="tpu_custom_call" | custom-call | tf_op jit(solution)/shard_map/pallas_call | solution.py:727
  164.2 2.2 %shard_map.103 = (f32[1,128]{1,0:T(1,128)}, f32[128,768]{1,0:T(8,128)}, f32[8,8,768]{2,1,0:T(8,128)}, f32[2,64,768]{2,1,0:T(8,128)}) custom-call(f32[1,128]{1,0:T(1,128)} %get-tuple-element.12.refs_0_, f32[128,768]{1,0:T(8,128)} %get-tuple-element.13.refs_1_, f32[8,8,768]{2,1,0:T(8,128)} %get-tuple-element.14.refs_2_, f32[2,64,768]{2,1,0:T(8,128)} %get-tuple-element.15.refs_3_), custom_call_target="tpu_custom_call" | custom-call | tf_op jit(solution)/shard_map/pallas_call | solution.py:737
